TPU v7x, 32 devices: a whole 2x2x4 slice. The times are simulated.
32 devices in a mesh: section: 8 (over y, x, core), uly: 4 (over z).
Axes of the slice: x: 2, y: 2, z: 4, core: 2. Of those that a mesh axis runs over, the one named last changes fastest.
Arguments:
- state: bfloat16 [8, 128, 3072], P('section', 'uly'), may hold values from -6 to 6
- patch_slot: int32 [8], replicated, may hold values from 0 to 3
- section_active: int32 [8], P('section'), may hold values from 1 to 2
- qkv_weight: bfloat16 [8, 3072, 3, 1536], P('section', None, None, 'uly'), may hold values from -0.109375 to 0.109375
- out_weight: bfloat16 [8, 1536, 3072], P('section', 'uly'), may hold values from -0.15625 to 0.15625
- norm_gain: bfloat16 [8, 3072], P('section'), may hold values from 0.099609375 to 1.8984375
- stale_keys: bfloat16 [8, 512, 1536], P('section', None, 'uly'), may hold values from -6 to 6
- stale_values: bfloat16 [8, 512, 1536], P('section', None, 'uly'), may hold values from -6 to 6
Outputs:
- final_state: bfloat16 [8, 128, 3072], P('section', 'uly')
All inputs are finite; a program needn't handle non-finite values.
Results may differ from a plain program's by a relative error of at most 0.019.
Values may be sent and summed in bfloat16 or wider, within the bound.
No kernel may reach another device: no remote copies, remote signals or barrier semaphores. Data moves between devices by JAX's collectives and lax.ppermute only.
A program may use at most 64 MiB of HBM per device.

v0:
```python
import functools
import math

import jax
import jax.numpy as jnp
from jax import lax
from jax.experimental import pallas as pl
from jax.experimental.pallas import tpu as pltpu
from jax.sharding import PartitionSpec as P

HD = 128
TICKS = 3
PASSES = 2
VMEM_LIMIT = 12 * 2**20
SCALE = HD ** (-0.5) * math.log2(math.e)
OUT_STEPS = 3
SHARES = (1, 1)


def row_spans(refs):
    start = 0
    for ref in refs:
        yield start, start + ref.shape[0], ref
        start += ref.shape[0]


def block_kernel(in_count, out_count, info, *refs):
    blocks = refs[:in_count]
    gain, w, wo, _, _ = refs[in_count:in_count + 5]
    terms = refs[in_count + 5:in_count + 5 + out_count]
    kc, vc, gained, attended = refs[in_count + 5 + out_count:]
    total_rows = gained.shape[0]
    heads = kc.shape[1] // HD

    @pl.when(info[1] > 0)
    def _():
        gain_row = gain[...].astype(jnp.float32)
        factors = []
        for first, end, block in row_spans(blocks):
            wide = block[...].astype(jnp.float32)
            mean_square = jnp.mean(wide * wide, axis=-1, keepdims=True)
            factors.append(lax.rsqrt(mean_square + 1e-06))
            gained[first:end, :] = (wide * gain_row).astype(jnp.bfloat16)
        projected = jnp.dot(gained[...], w[...], preferred_element_type=jnp.float32)
        projected = (projected * jnp.concatenate(factors)).astype(jnp.bfloat16)
        width = heads * HD
        start = pl.multiple_of(info[0], total_rows)
        kc[pl.ds(start, total_rows), :] = projected[:, width:2 * width]
        vc[pl.ds(start, total_rows), :] = projected[:, 2 * width:]
        for h in range(heads):
            cols = pl.ds(h * HD, HD)
            scores = lax.dot_general(
                projected[:, h * HD:(h + 1) * HD],
                kc[:, cols],
                (((1,), (1,)), ((), ())),
                preferred_element_type=jnp.float32,
            )
            top = jnp.max(scores, axis=-1, keepdims=True)
            weights = jnp.exp2((scores - top) * SCALE)
            share = 1.0 / jnp.sum(weights, axis=-1, keepdims=True)
            mixed = jnp.dot(
                weights.astype(jnp.bfloat16), vc[:, cols], preferred_element_type=jnp.float32
            )
            attended[:, cols] = (mixed * share).astype(jnp.bfloat16)
        step = wo.shape[1] // OUT_STEPS
        for i in range(OUT_STEPS):
            cols = pl.ds(i * step, step)
            product = jnp.dot(
                attended[...], wo[:, cols], preferred_element_type=jnp.float32
            ).astype(jnp.bfloat16)
            for first, end, term in row_spans(terms):
                term[:, cols] = product[first:end]

    @pl.when(info[1] <= 0)
    def _():
        for term in terms:
            term[...] = jnp.zeros_like(term)


def load_kernel(w_hbm, wo_hbm, kc_hbm, vc_hbm, gain_hbm, w, wo, kc, vc, gain, sems):
    parts, _, width = w_hbm.shape
    pairs = [(w_hbm.at[i], w.at[:, pl.ds(i * width, width)]) for i in range(parts)]
    pairs += [(wo_hbm, wo), (kc_hbm, kc), (vc_hbm, vc), (gain_hbm, gain)]
    copies = [pltpu.make_async_copy(a, b, sems.at[i]) for i, (a, b) in enumerate(pairs)]
    for copy in copies:
        copy.start()
    for copy in copies:
        copy.wait()


def loaded(w, wo, kc, vc, gain):
    parts, depth, width = w.shape
    arrays = (w, wo, kc, vc, gain)
    shapes = [(depth, parts * width)] + [a.shape for a in arrays[1:]]
    return pl.pallas_call(
        load_kernel,
        out_shape=[pltpu.VMEM(shape, w.dtype) for shape in shapes],
        in_specs=[pl.BlockSpec(memory_space=pl.ANY)] * len(arrays),
        out_specs=[pl.BlockSpec(memory_space=pltpu.VMEM)] * len(arrays),
        scratch_shapes=[pltpu.SemaphoreType.DMA((parts + 4,))],
        compiler_params=pltpu.CompilerParams(vmem_limit_bytes=VMEM_LIMIT),
        cost_estimate=pl.CostEstimate(
            flops=0, bytes_accessed=2 * sum(a.size for a in arrays), transcendentals=0
        ),
    )(*[pltpu.with_memory_space_constraint(a, pltpu.HBM) for a in arrays])


def block_terms(info, blocks, rows_out, gain, w, wo, kc, vc):
    count, width = len(blocks), blocks[0].shape[1]
    row_count = sum(rows_out)
    vmem = pl.BlockSpec(memory_space=pltpu.VMEM)
    flops = 2 * row_count * (w.size + wo.size + 2 * kc.size)
    held = [pltpu.with_memory_space_constraint(x, pltpu.VMEM) for x in (gain, w, wo, kc, vc)]
    cache = pltpu.VMEM(kc.shape, kc.dtype)
    out = pl.pallas_call(
        functools.partial(block_kernel, count, len(rows_out)),
        out_shape=[jax.ShapeDtypeStruct((rows, width), jnp.bfloat16) for rows in rows_out]
        + [cache] * 2,
        in_specs=[pl.BlockSpec(memory_space=pltpu.SMEM)] + [vmem] * (count + 5),
        out_specs=[vmem] * (len(rows_out) + 2),
        input_output_aliases={count + 4: len(rows_out), count + 5: len(rows_out) + 1},
        scratch_shapes=[
            pltpu.VMEM((row_count, width), jnp.bfloat16),
            pltpu.VMEM((row_count, kc.shape[1]), jnp.bfloat16),
        ],
        compiler_params=pltpu.CompilerParams(vmem_limit_bytes=VMEM_LIMIT),
        cost_estimate=pl.CostEstimate(
            flops=flops, bytes_accessed=2 * (w.size + wo.size), transcendentals=0
        ),
    )(info, *blocks, *held)
    return out[:-2], out[-2], out[-1]


STAY = ((0, 0), (1, 1), (2, 2), (3, 3))
NEAR = ((0, 1), (1, 0), (2, 3), (3, 2))
FAR = ((0, 3), (1, 2), (2, 1), (3, 0))
CROSS = ((0, 2), (1, 3), (2, 0), (3, 1))


def send(block, pairs, hop=0):
    sections = lax.axis_size("section")
    n = lax.axis_size("uly")
    route = [
        (s * n + a, (s + hop) % sections * n + b) for s in range(sections) for a, b in pairs
    ]
    return lax.ppermute(block, ("section", "uly"), route)


def summed(*blocks):
    total = blocks[0].astype(jnp.float32)
    for block in blocks[1:]:
        total = total + block.astype(jnp.float32)
    return total


def summed(*blocks):
    total = blocks[0].astype(jnp.float32)
    for block in blocks[1:]:
        total = total + block.astype(jnp.float32)
    return total


def rounded(*blocks):
    return summed(*blocks).astype(jnp.bfloat16)


def behind(block, other):
    return lax.optimization_barrier((block, other))[0]


def pieces_of(rows):
    return [rows * share // sum(SHARES) for share in SHARES]


def cut(blocks, sizes):
    whole = jnp.concatenate(blocks)
    starts = [sum(sizes[:i]) for i in range(len(sizes))]
    return [whole[start:start + size] for start, size in zip(starts, sizes)]


def gathered(own, low):
    far = send(own, FAR)
    near = send(own, NEAR)
    last = send(far, NEAR)
    kept = [jnp.where(low, own, far), jnp.where(low, far, own)]
    return kept, [jnp.where(low, near, last), jnp.where(low, last, near)]


def passed_on(kept, terms, hop):
    count = len(kept)
    next_kept, next_others = [], []
    pair = None
    for current, mine, partners in zip(kept, terms[:count], terms[count:]):
        partners = partners if pair is None else behind(partners, pair)
        pair = rounded(mine, send(partners, NEAR))
        updated = rounded(current, pair, send(pair, FAR))
        next_others.append(send(updated, NEAR, hop))
        next_kept.append(send(updated, STAY, hop) if hop else updated)
    return next_kept, next_others


def delivered(kept, terms, low):
    first, second, near_first, near_second = terms
    before = jnp.where(low, *cut(kept, [first.shape[0], second.shape[0]]))
    cross = send(jnp.where(low, near_second, near_first), CROSS, 1)
    far = send(jnp.where(low, second, first), FAR, 1)
    near = send(jnp.where(low, near_first, near_second), NEAR, 1)
    base = send(rounded(before, jnp.where(low, first, second)), STAY, 1)
    return rounded(base, near, far, cross)


def shards(
    state, patch_slot, section_active, qkv_weight, out_weight, norm_gain, stale_keys, stale_values
):
    section_count = lax.axis_size("section")
    section_index = lax.axis_index("section")
    block_count = section_active[0]
    n = lax.axis_size("uly")
    low = lax.axis_index("uly") < n // 2
    shard_rows = state.shape[1]
    patch_rows = shard_rows * n
    stored = (
        jnp.transpose(qkv_weight[0], (1, 0, 2)),
        out_weight[0],
        stale_keys[0],
        stale_values[0],
        norm_gain,
    )
    w, wo, kc, vc, gain = loaded(*stored)
    kept, others = gathered(state[0], low)
    sizes = pieces_of(patch_rows // 2)
    for tick in range(TICKS):
        slot = patch_slot[(section_index - tick) % section_count]
        for index in range(PASSES):
            applies = block_count > index
            info = jnp.stack([slot * patch_rows, applies.astype(jnp.int32)])
            last = index == PASSES - 1
            final = last and tick == TICKS - 1
            rows_out = [shard_rows] * n if final else sizes * 2
            terms, kc, vc = block_terms(info, kept + others, rows_out, gain, w, wo, kc, vc)
            if final:
                return delivered(kept, terms, low)[None]
            kept = cut(kept, sizes) if tick + index == 0 else kept
            kept, others = passed_on(kept, terms, 1 if last else 0)


def solution(mesh):
    return jax.shard_map(
        shards,
        mesh=mesh,
        in_specs=(
            P("section", "uly", None),
            P(),
            P("section"),
            P("section", None, None, "uly"),
            P("section", "uly", None),
            P("section", None),
            P("section", None, "uly"),
            P("section", None, "uly"),
        ),
        out_specs=P("section", "uly", None),
        check_vma=False,
    )
```

profile of v0, /device:TPU:14, one launch (start us, length us, event | category | flops | bytes accessed | tf_op | source)
XLA Modules:
  0.0 218.4 jit_solution(16454331568197097199)
XLA Ops:
  6.8 3.9 %shard_map.82 = (bf16[3072,1152]{1,0:T(8,128)(2,1)S(1)}, bf16[384,3072]{1,0:T(8,128)(2,1)S(1)}, bf16[512,384]{1,0:T(8,128)(2,1)S(1)}, bf16[512,384]{1,0:T(8,128)(2,1)S(1)}, bf16[1,3072]{1,0:T(2,128)(2,1)S(1)}) custom-call(bf16[3,3072,384]{2,1,0:T(8,128)(2,1)} %bitcast.11, bf16[384,3072]{1,0:T(8,128)(2,1)} %bitcast.12, bf16[512,384]{1,0:T(8,128)(2,1)} %bitcast.13, ...), custom_call_target="tpu_custom_call" | custom-call | bytes 10229760 | tf_op jit(solution)/shard_map/pallas_call | solution.py:95
  13.5 3.9 %collective-permute-done.2 = bf16[32,3072]{1,0:T(8,128)(2,1)S(1)} collective-permute-done((bf16[32,3072]{1,0:T(8,128)(2,1)S(1)}, bf16[32,3072]{1,0:T(8,128)(2,1)S(1)}, u32[]{:S(2)}, u32[]{:S(2)}) %collective-permute-start.2) | collective-permute-done | bytes 196640 | tf_op jit(solution)/shard_map/ppermute | solution.py:146
  17.4 3.0 %shard_map.83 = (bf16[32,3072]{1,0:T(8,128)(2,1)S(1)}, bf16[32,3072]{1,0:T(8,128)(2,1)S(1)}, bf16[32,3072]{1,0:T(8,128)(2,1)S(1)}, bf16[32,3072]{1,0:T(8,128)(2,...) custom-call(s32[2]{0:T(128)S(1)} %pad_add_fusion.1.info, ...), custom_call_target="tpu_custom_call", output_to_operand_aliasing={{4}: (8, {}), {5}: (9, {})} | custom-call | flops 1308622848 | bytes 9437184 | tf_op jit(solution)/shard_map/pallas_call | solution.py:115
  20.9 5.3 %collective-permute-done.3 = bf16[32,3072]{1,0:T(8,128)(2,1)S(1)} collective-permute-done((bf16[32,3072]{1,0:T(8,128)(2,1)S(1)}, bf16[32,3072]{1,0:T(8,128)(2,1)S(1)}, u32[]{:S(2)}, u32[]{:S(2)}) %collective-permute-start.3) | collective-permute-done | bytes 196640 | tf_op jit(solution)/shard_map/ppermute | solution.py:146
  28.0 6.2 %collective-permute-done.5 = bf16[32,3072]{1,0:T(8,128)(2,1)S(1)} collective-permute-done((bf16[32,3072]{1,0:T(8,128)(2,1)S(1)}, bf16[32,3072]{1,0:T(8,128)(2,1)S(1)}, u32[]{:S(2)}, u32[]{:S(2)}) %collective-permute-start.5) | collective-permute-done | bytes 196640 | tf_op jit(solution)/shard_map/ppermute | solution.py:146
  34.6 4.9 %collective-permute-done.4 = bf16[32,3072]{1,0:T(8,128)(2,1)S(1)} collective-permute-done((bf16[32,3072]{1,0:T(8,128)(2,1)S(1)}, bf16[32,3072]{1,0:T(8,128)(2,1)S(1)}, u32[]{:S(2)}, u32[]{:S(2)}) %collective-permute-start.4) | collective-permute-done | bytes 196640 | tf_op jit(solution)/shard_map/ppermute | solution.py:146
  39.7 4.3 %collective-permute-done.6 = bf16[32,3072]{1,0:T(8,128)(2,1)S(1)} collective-permute-done((bf16[32,3072]{1,0:T(8,128)(2,1)S(1)}, bf16[32,3072]{1,0:T(8,128)(2,1)S(1)}, u32[]{:S(2)}, u32[]{:S(2)}) %collective-permute-start.6) | collective-permute-done | bytes 196640 | tf_op jit(solution)/shard_map/ppermute | solution.py:146
  45.5 4.3 %collective-permute-done.8.refs_3_ = bf16[32,3072]{1,0:T(8,128)(2,1)S(1)} collective-permute-done((bf16[32,3072]{1,0:T(8,128)(2,1)S(1)}, bf16[32,3072]{1,0:T(8,128)(2,1)S(1)}, u32[]{:S(2)}, u32[]{:S(2)}) %collective-permute-start.8) | collective-permute-done | bytes 196640 | tf_op jit(solution)/shard_map/ppermute | solution.py:146
  49.8 3.0 %shard_map.84 = (bf16[32,3072]{1,0:T(8,128)(2,1)S(1)}, bf16[32,3072]{1,0:T(8,128)(2,1)S(1)}, bf16[32,3072]{1,0:T(8,128)(2,1)S(1)}, bf16[32,3072]{1,0:T(8,128)(2,...) custom-call(s32[2]{0:T(128)S(1)} %pad_add_fusion.info, ...), custom_call_target="tpu_custom_call", output_to_operand_aliasing={{4}: (8, {}), {5}: (9, {})} | custom-call | flops 1308622848 | bytes 9437184 | tf_op jit(solution)/shard_map/pallas_call | solution.py:115
  53.0 7.8 %collective-permute-done.9 = bf16[32,3072]{1,0:T(8,128)(2,1)S(1)} collective-permute-done((bf16[32,3072]{1,0:T(8,128)(2,1)S(1)}, bf16[32,3072]{1,0:T(8,128)(2,1)S(1)}, u32[]{:S(2)}, u32[]{:S(2)}) %collective-permute-start.9) | collective-permute-done | bytes 196640 | tf_op jit(solution)/shard_map/ppermute | solution.py:146
  60.9 3.9 %collective-permute-start.10 = (bf16[32,3072]{1,0:T(8,128)(2,1)S(1)}, bf16[32,3072]{1,0:T(8,128)(2,1)S(1)}, u32[]{:S(2)}, u32[]{:S(2)}) collective-permute-start(bf16[32,3072]{1,0:T(8,128)(2,1)S(1)} %add_convert_fusion.17), channel_id=1, source_target_pairs={{0,3},{1,2},{2,1},{3,0},{4,7},{5,6},{6,5},{7,4},{8,11},{9,10},{10,... | collective-permute-start | bytes 589832 | tf_op jit(solution)/shard_map/ppermute | solution.py:146
  64.8 3.8 %collective-permute-done.12 = bf16[32,3072]{1,0:T(8,128)(2,1)S(1)} collective-permute-done((bf16[32,3072]{1,0:T(8,128)(2,1)S(1)}, bf16[32,3072]{1,0:T(8,128)(2,1)S(1)}, u32[]{:S(2)}, u32[]{:S(2)}) %collective-permute-start.12) | collective-permute-done | bytes 196640 | tf_op jit(solution)/shard_map/ppermute | solution.py:146
  68.7 3.2 %collective-permute-start.13 = (bf16[32,3072]{1,0:T(8,128)(2,1)S(1)}, bf16[32,3072]{1,0:T(8,128)(2,1)S(1)}, u32[]{:S(2)}, u32[]{:S(2)}) collective-permute-start(bf16[32,3072]{1,0:T(8,128)(2,1)S(1)} %add_convert_fusion.15), channel_id=1, source_target_pairs={{0,3},{1,2},{2,1},{3,0},{4,7},{5,6},{6,5},{7,4},{8,11},{9,10},{10,... | collective-permute-start | bytes 589832 | tf_op jit(solution)/shard_map/ppermute | solution.py:146
  72.1 5.5 %collective-permute-done.13 = bf16[32,3072]{1,0:T(8,128)(2,1)S(1)} collective-permute-done((bf16[32,3072]{1,0:T(8,128)(2,1)S(1)}, bf16[32,3072]{1,0:T(8,128)(2,1)S(1)}, u32[]{:S(2)}, u32[]{:S(2)}) %collective-permute-start.13) | collective-permute-done | bytes 196640 | tf_op jit(solution)/shard_map/ppermute | solution.py:146
  81.1 3.9 %collective-permute-done.16.refs_3_ = bf16[32,3072]{1,0:T(8,128)(2,1)S(1)} collective-permute-done((bf16[32,3072]{1,0:T(8,128)(2,1)S(1)}, bf16[32,3072]{1,0:T(8,128)(2,1)S(1)}, u32[]{:S(2)}, u32[]{:S(2)}) %collective-permute-start.16) | collective-permute-done | bytes 196640 | tf_op jit(solution)/shard_map/ppermute | solution.py:146
  91.0 5.4 %collective-permute-done.17 = bf16[32,3072]{1,0:T(8,128)(2,1)S(1)} collective-permute-done((bf16[32,3072]{1,0:T(8,128)(2,1)S(1)}, bf16[32,3072]{1,0:T(8,128)(2,1)S(1)}, u32[]{:S(2)}, u32[]{:S(2)}) %collective-permute-start.17) | collective-permute-done | bytes 196640 | tf_op jit(solution)/shard_map/ppermute | solution.py:146
  96.8 5.1 %collective-permute-start.18 = (bf16[32,3072]{1,0:T(8,128)(2,1)S(1)}, bf16[32,3072]{1,0:T(8,128)(2,1)S(1)}, u32[]{:S(2)}, u32[]{:S(2)}) collective-permute-start(bf16[32,3072]{1,0:T(8,128)(2,1)S(1)} %add_convert_fusion.13), channel_id=1, source_target_pairs={{0,3},{1,2},{2,1},{3,0},{4,7},{5,6},{6,5},{7,4},{8,11},{9,10},{10,... | collective-permute-start | bytes 589832 | tf_op jit(solution)/shard_map/ppermute | solution.py:146
  104.4 7.0 %collective-permute-start.20 = (bf16[32,3072]{1,0:T(8,128)(2,1)S(1)}, bf16[32,3072]{1,0:T(8,128)(2,1)S(1)}, u32[]{:S(2)}, u32[]{:S(2)}) collective-permute-start(bf16[32,3072]{1,0:T(8,128)(2,1)S(1)} %add_convert_fusion.11), channel_id=1, source_target_pairs={{0,3},{1,2},{2,1},{3,0},{4,7},{5,6},{6,5},{7,4},{8,11},{9,10},{10,... | collective-permute-start | bytes 589832 | tf_op jit(solution)/shard_map/ppermute | solution.py:146
  111.8 3.2 %collective-permute-start.21 = (bf16[32,3072]{1,0:T(8,128)(2,1)S(1)}, bf16[32,3072]{1,0:T(8,128)(2,1)S(1)}, u32[]{:S(2)}, u32[]{:S(2)}) collective-permute-start(bf16[32,3072]{1,0:T(8,128)(2,1)S(1)} %add_convert_fusion.12.refs_0_), channel_id=1, source_target_pairs={{0,1},{1,0},{2,3},{3,2},{4,5},{5,4},{6,7},{7,6},{8,9},{9,8},{10,11... | collective-permute-start | bytes 589832 | tf_op jit(solution)/shard_map/ppermute | solution.py:146
  115.4 5.1 %collective-permute-start.22 = (bf16[32,3072]{1,0:T(8,128)(2,1)S(1)}, bf16[32,3072]{1,0:T(8,128)(2,1)S(1)}, u32[]{:S(2)}, u32[]{:S(2)}) collective-permute-start(bf16[32,3072]{1,0:T(8,128)(2,1)S(1)} %add_convert_fusion.10.refs_1_), channel_id=1, source_target_pairs={{0,1},{1,0},{2,3},{3,2},{4,5},{5,4},{6,7},{7,6},{8,9},{9,8},{10,11... | collective-permute-start | bytes 589832 | tf_op jit(solution)/shard_map/ppermute | solution.py:146
  121.5 3.5 %collective-permute-done.22.refs_3_ = bf16[32,3072]{1,0:T(8,128)(2,1)S(1)} collective-permute-done((bf16[32,3072]{1,0:T(8,128)(2,1)S(1)}, bf16[32,3072]{1,0:T(8,128)(2,1)S(1)}, u32[]{:S(2)}, u32[]{:S(2)}) %collective-permute-start.22) | collective-permute-done | bytes 196640 | tf_op jit(solution)/shard_map/ppermute | solution.py:146
  125.0 3.2 %shard_map.86 = (bf16[32,3072]{1,0:T(8,128)(2,1)S(1)}, bf16[32,3072]{1,0:T(8,128)(2,1)S(1)}, bf16[32,3072]{1,0:T(8,128)(2,1)S(1)}, bf16[32,3072]{1,0:T(8,128)(2,...) custom-call(s32[2]{0:T(128)S(1)} %pad_add_fusion.2.info, ...), custom_call_target="tpu_custom_call", output_to_operand_aliasing={{4}: (8, {}), {5}: (9, {})} | custom-call | flops 1308622848 | bytes 9437184 | tf_op jit(solution)/shard_map/pallas_call | solution.py:115
  129.5 6.5 %collective-permute-done.23 = bf16[32,3072]{1,0:T(8,128)(2,1)S(1)} collective-permute-done((bf16[32,3072]{1,0:T(8,128)(2,1)S(1)}, bf16[32,3072]{1,0:T(8,128)(2,1)S(1)}, u32[]{:S(2)}, u32[]{:S(2)}) %collective-permute-start.23) | collective-permute-done | bytes 196640 | tf_op jit(solution)/shard_map/ppermute | solution.py:146
  138.1 3.6 %collective-permute-done.26 = bf16[32,3072]{1,0:T(8,128)(2,1)S(1)} collective-permute-done((bf16[32,3072]{1,0:T(8,128)(2,1)S(1)}, bf16[32,3072]{1,0:T(8,128)(2,1)S(1)}, u32[]{:S(2)}, u32[]{:S(2)}) %collective-permute-start.26) | collective-permute-done | bytes 196640 | tf_op jit(solution)/shard_map/ppermute | solution.py:146
  145.8 3.5 %collective-permute-done.27 = bf16[32,3072]{1,0:T(8,128)(2,1)S(1)} collective-permute-done((bf16[32,3072]{1,0:T(8,128)(2,1)S(1)}, bf16[32,3072]{1,0:T(8,128)(2,1)S(1)}, u32[]{:S(2)}, u32[]{:S(2)}) %collective-permute-start.27) | collective-permute-done | bytes 196640 | tf_op jit(solution)/shard_map/ppermute | solution.py:146
  150.1 3.5 %collective-permute-done.29.refs_2_ = bf16[32,3072]{1,0:T(8,128)(2,1)S(1)} collective-permute-done((bf16[32,3072]{1,0:T(8,128)(2,1)S(1)}, bf16[32,3072]{1,0:T(8,128)(2,1)S(1)}, u32[]{:S(2)}, u32[]{:S(2)}) %collective-permute-start.29) | collective-permute-done | bytes 196640 | tf_op jit(solution)/shard_map/ppermute | solution.py:146
  163.5 5.0 %collective-permute-done.31 = bf16[32,3072]{1,0:T(8,128)(2,1)S(1)} collective-permute-done((bf16[32,3072]{1,0:T(8,128)(2,1)S(1)}, bf16[32,3072]{1,0:T(8,128)(2,1)S(1)}, u32[]{:S(2)}, u32[]{:S(2)}) %collective-permute-start.31) | collective-permute-done | bytes 196640 | tf_op jit(solution)/shard_map/ppermute | solution.py:146
  174.8 5.5 %collective-permute-start.34 = (bf16[32,3072]{1,0:T(8,128)(2,1)S(1)}, bf16[32,3072]{1,0:T(8,128)(2,1)S(1)}, u32[]{:S(2)}, u32[]{:S(2)}) collective-permute-start(bf16[32,3072]{1,0:T(8,128)(2,1)S(1)} %add_convert_fusion.3), channel_id=1, source_target_pairs={{0,3},{1,2},{2,1},{3,0},{4,7},{5,6},{6,5},{7,4},{8,11},{9,10},{10,... | collective-permute-start | bytes 589832 | tf_op jit(solution)/shard_map/ppermute | solution.py:146
  184.1 4.1 %collective-permute-start.36 = (bf16[32,3072]{1,0:T(8,128)(2,1)S(1)}, bf16[32,3072]{1,0:T(8,128)(2,1)S(1)}, u32[]{:S(2)}, u32[]{:S(2)}) collective-permute-start(bf16[32,3072]{1,0:T(8,128)(2,1)S(1)} %add_convert_fusion.2.refs_1_), channel_id=1, source_target_pairs={{0,1},{1,0},{2,3},{3,2},{4,5},{5,4},{6,7},{7,6},{8,9},{9,8},{10,11... | collective-permute-start | bytes 589832 | tf_op jit(solution)/shard_map/ppermute | solution.py:146
  198.1 4.4 %collective-permute-done.38 = bf16[32,3072]{1,0:T(8,128)(2,1)S(1)} collective-permute-done((bf16[32,3072]{1,0:T(8,128)(2,1)S(1)}, bf16[32,3072]{1,0:T(8,128)(2,1)S(1)}, u32[]{:S(2)}, u32[]{:S(2)}) %collective-permute-start.38) | collective-permute-done | bytes 196640 | tf_op jit(solution)/shard_map/ppermute | solution.py:146
  202.6 6.9 %collective-permute-done.40 = bf16[32,3072]{1,0:T(8,128)(2,1)S(1)} collective-permute-done((bf16[32,3072]{1,0:T(8,128)(2,1)S(1)}, bf16[32,3072]{1,0:T(8,128)(2,1)S(1)}, u32[]{:S(2)}, u32[]{:S(2)}) %collective-permute-start.40) | collective-permute-done | bytes 196640 | tf_op jit(solution)/shard_map/ppermute | solution.py:146
  209.5 8.1 %collective-permute-done.39 = bf16[32,3072]{1,0:T(8,128)(2,1)S(1)} collective-permute-done((bf16[32,3072]{1,0:T(8,128)(2,1)S(1)}, bf16[32,3072]{1,0:T(8,128)(2,1)S(1)}, u32[]{:S(2)}, u32[]{:S(2)}) %collective-permute-start.39) | collective-permute-done | bytes 196640 | tf_op jit(solution)/shard_map/ppermute | solution.py:146
  (92 shorter events, 64.9 us)
Async XLA Ops:
  0.0 11.1 %collective-permute-start = (bf16[32,3072]{1,0:T(8,128)(2,1)}, bf16[32,3072]{1,0:T(8,128)(2,1)S(1)}, u32[]{:S(2)}, u32[]{:S(2)}) collective-permute-start(bf16[32,3072]{1,0:T(8,128)(2,1)} %bitcast.15), channel_id=1, source_target_pairs={{0,3},{1,2},{2,1},{3,0},{4,7},{5,6},{6,5},{7,4},{8,11},{9,10},{10,... | collective-permute-start | bytes 589832 | tf_op jit(solution)/shard_map/ppermute | solution.py:146
  1.6 11.9 %collective-permute-start.1 = (bf16[32,3072]{1,0:T(8,128)(2,1)}, bf16[32,3072]{1,0:T(8,128)(2,1)S(1)}, u32[]{:S(2)}, u32[]{:S(2)}) collective-permute-start(bf16[32,3072]{1,0:T(8,128)(2,1)} %bitcast.16), channel_id=1, source_target_pairs={{0,1},{1,0},{2,3},{3,2},{4,5},{5,4},{6,7},{7,6},{8,9},{9,8},{10,11... | collective-permute-start | bytes 589832 | tf_op jit(solution)/shard_map/ppermute | solution.py:146
  26.2 7.9 %collective-permute-start.5 = (bf16[32,3072]{1,0:T(8,128)(2,1)S(1)}, bf16[32,3072]{1,0:T(8,128)(2,1)S(1)}, u32[]{:S(2)}, u32[]{:S(2)}) collective-permute-start(bf16[32,3072]{1,0:T(8,128)(2,1)S(1)} %get-tuple-element.58), channel_id=1, source_target_pairs={{0,1},{1,0},{2,3},{3,2},{4,5},{5,4},{6,7},{7,6},{8,9},{9,8},{10,11... | collective-permute-start | bytes 589832 | tf_op jit(solution)/shard_map/ppermute | solution.py:146
  26.8 12.7 %collective-permute-start.4 = (bf16[32,3072]{1,0:T(8,128)(2,1)S(1)}, bf16[32,3072]{1,0:T(8,128)(2,1)S(1)}, u32[]{:S(2)}, u32[]{:S(2)}) collective-permute-start(bf16[32,3072]{1,0:T(8,128)(2,1)S(1)} %add_convert_fusion.21), channel_id=1, source_target_pairs={{0,3},{1,2},{2,1},{3,0},{4,7},{5,6},{6,5},{7,4},{8,11},{9,10},{10,... | collective-permute-start | bytes 589832 | tf_op jit(solution)/shard_map/ppermute | solution.py:146
  34.2 9.8 %collective-permute-start.6 = (bf16[32,3072]{1,0:T(8,128)(2,1)S(1)}, bf16[32,3072]{1,0:T(8,128)(2,1)S(1)}, u32[]{:S(2)}, u32[]{:S(2)}) collective-permute-start(bf16[32,3072]{1,0:T(8,128)(2,1)S(1)} %add_convert_fusion.19), channel_id=1, source_target_pairs={{0,3},{1,2},{2,1},{3,0},{4,7},{5,6},{6,5},{7,4},{8,11},{9,10},{10,... | collective-permute-start | bytes 589832 | tf_op jit(solution)/shard_map/ppermute | solution.py:146
  52.9 7.9 %collective-permute-start.9 = (bf16[32,3072]{1,0:T(8,128)(2,1)S(1)}, bf16[32,3072]{1,0:T(8,128)(2,1)S(1)}, u32[]{:S(2)}, u32[]{:S(2)}) collective-permute-start(bf16[32,3072]{1,0:T(8,128)(2,1)S(1)} %get-tuple-element.62), channel_id=1, source_target_pairs={{0,1},{1,0},{2,3},{3,2},{4,5},{5,4},{6,7},{7,6},{8,9},{9,8},{10,11... | collective-permute-start | bytes 589832 | tf_op jit(solution)/shard_map/ppermute | solution.py:146
  60.8 7.8 %collective-permute-start.12 = (bf16[32,3072]{1,0:T(8,128)(2,1)S(1)}, bf16[32,3072]{1,0:T(8,128)(2,1)S(1)}, u32[]{:S(2)}, u32[]{:S(2)}) collective-permute-start(bf16[32,3072]{1,0:T(8,128)(2,1)S(1)} %get-tuple-element.65), channel_id=1, source_target_pairs={{0,1},{1,0},{2,3},{3,2},{4,5},{5,4},{6,7},{7,6},{8,9},{9,8},{10,11... | collective-permute-start | bytes 589832 | tf_op jit(solution)/shard_map/ppermute | solution.py:146
  60.9 11.0 %collective-permute-start.10 = (bf16[32,3072]{1,0:T(8,128)(2,1)S(1)}, bf16[32,3072]{1,0:T(8,128)(2,1)S(1)}, u32[]{:S(2)}, u32[]{:S(2)}) collective-permute-start(bf16[32,3072]{1,0:T(8,128)(2,1)S(1)} %add_convert_fusion.17), channel_id=1, source_target_pairs={{0,3},{1,2},{2,1},{3,0},{4,7},{5,6},{6,5},{7,4},{8,11},{9,10},{10,... | collective-permute-start | bytes 589832 | tf_op jit(solution)/shard_map/ppermute | solution.py:146
  68.7 8.9 %collective-permute-start.13 = (bf16[32,3072]{1,0:T(8,128)(2,1)S(1)}, bf16[32,3072]{1,0:T(8,128)(2,1)S(1)}, u32[]{:S(2)}, u32[]{:S(2)}) collective-permute-start(bf16[32,3072]{1,0:T(8,128)(2,1)S(1)} %add_convert_fusion.15), channel_id=1, source_target_pairs={{0,3},{1,2},{2,1},{3,0},{4,7},{5,6},{6,5},{7,4},{8,11},{9,10},{10,... | collective-permute-start | bytes 589832 | tf_op jit(solution)/shard_map/ppermute | solution.py:146
  72.0 8.3 %collective-permute-start.15 = (bf16[32,3072]{1,0:T(8,128)(2,1)S(1)}, bf16[32,3072]{1,0:T(8,128)(2,1)S(1)}, u32[]{:S(2)}, u32[]{:S(2)}) collective-permute-start(bf16[32,3072]{1,0:T(8,128)(2,1)S(1)} %add_convert_fusion.16), channel_id=1, source_target_pairs={{0,5},{1,4},{2,7},{3,6},{4,9},{5,8},{6,11},{7,10},{8,13},{9,12},{1... | collective-permute-start | bytes 589832 | tf_op jit(solution)/shard_map/ppermute | solution.py:146
  72.0 9.1 %collective-permute-start.11 = (bf16[32,3072]{1,0:T(8,128)(2,1)S(1)}, bf16[32,3072]{1,0:T(8,128)(2,1)S(1)}, u32[]{:S(2)}, u32[]{:S(2)}) collective-permute-start(bf16[32,3072]{1,0:T(8,128)(2,1)S(1)} %add_convert_fusion.16), channel_id=1, source_target_pairs={{0,4},{1,5},{2,6},{3,7},{4,8},{5,9},{6,10},{7,11},{8,12},{9,13},{1... | collective-permute-start | bytes 589832 | tf_op jit(solution)/shard_map/ppermute | solution.py:146
  77.8 8.8 %collective-permute-start.14 = (bf16[32,3072]{1,0:T(8,128)(2,1)S(1)}, bf16[32,3072]{1,0:T(8,128)(2,1)S(1)}, u32[]{:S(2)}, u32[]{:S(2)}) collective-permute-start(bf16[32,3072]{1,0:T(8,128)(2,1)S(1)} %add_convert_fusion.14), channel_id=1, source_target_pairs={{0,4},{1,5},{2,6},{3,7},{4,8},{5,9},{6,10},{7,11},{8,12},{9,13},{1... | collective-permute-start | bytes 589832 | tf_op jit(solution)/shard_map/ppermute | solution.py:146
  96.5 7.9 %collective-permute-start.19 = (bf16[32,3072]{1,0:T(8,128)(2,1)S(1)}, bf16[32,3072]{1,0:T(8,128)(2,1)S(1)}, u32[]{:S(2)}, u32[]{:S(2)}) collective-permute-start(bf16[32,3072]{1,0:T(8,128)(2,1)S(1)} %get-tuple-element.72), channel_id=1, source_target_pairs={{0,1},{1,0},{2,3},{3,2},{4,5},{5,4},{6,7},{7,6},{8,9},{9,8},{10,11... | collective-permute-start | bytes 589832 | tf_op jit(solution)/shard_map/ppermute | solution.py:146
  96.8 14.9 %collective-permute-start.18 = (bf16[32,3072]{1,0:T(8,128)(2,1)S(1)}, bf16[32,3072]{1,0:T(8,128)(2,1)S(1)}, u32[]{:S(2)}, u32[]{:S(2)}) collective-permute-start(bf16[32,3072]{1,0:T(8,128)(2,1)S(1)} %add_convert_fusion.13), channel_id=1, source_target_pairs={{0,3},{1,2},{2,1},{3,0},{4,7},{5,6},{6,5},{7,4},{8,11},{9,10},{10,... | collective-permute-start | bytes 589832 | tf_op jit(solution)/shard_map/ppermute | solution.py:146
  104.4 10.9 %collective-permute-start.20 = (bf16[32,3072]{1,0:T(8,128)(2,1)S(1)}, bf16[32,3072]{1,0:T(8,128)(2,1)S(1)}, u32[]{:S(2)}, u32[]{:S(2)}) collective-permute-start(bf16[32,3072]{1,0:T(8,128)(2,1)S(1)} %add_convert_fusion.11), channel_id=1, source_target_pairs={{0,3},{1,2},{2,1},{3,0},{4,7},{5,6},{6,5},{7,4},{8,11},{9,10},{10,... | collective-permute-start | bytes 589832 | tf_op jit(solution)/shard_map/ppermute | solution.py:146
  111.8 9.7 %collective-permute-start.21 = (bf16[32,3072]{1,0:T(8,128)(2,1)S(1)}, bf16[32,3072]{1,0:T(8,128)(2,1)S(1)}, u32[]{:S(2)}, u32[]{:S(2)}) collective-permute-start(bf16[32,3072]{1,0:T(8,128)(2,1)S(1)} %add_convert_fusion.12.refs_0_), channel_id=1, source_target_pairs={{0,1},{1,0},{2,3},{3,2},{4,5},{5,4},{6,7},{7,6},{8,9},{9,8},{10,11... | collective-permute-start | bytes 589832 | tf_op jit(solution)/shard_map/ppermute | solution.py:146
  115.4 9.6 %collective-permute-start.22 = (bf16[32,3072]{1,0:T(8,128)(2,1)S(1)}, bf16[32,3072]{1,0:T(8,128)(2,1)S(1)}, u32[]{:S(2)}, u32[]{:S(2)}) collective-permute-start(bf16[32,3072]{1,0:T(8,128)(2,1)S(1)} %add_convert_fusion.10.refs_1_), channel_id=1, source_target_pairs={{0,1},{1,0},{2,3},{3,2},{4,5},{5,4},{6,7},{7,6},{8,9},{9,8},{10,11... | collective-permute-start | bytes 589832 | tf_op jit(solution)/shard_map/ppermute | solution.py:146
  128.3 7.7 %collective-permute-start.23 = (bf16[32,3072]{1,0:T(8,128)(2,1)S(1)}, bf16[32,3072]{1,0:T(8,128)(2,1)S(1)}, u32[]{:S(2)}, u32[]{:S(2)}) collective-permute-start(bf16[32,3072]{1,0:T(8,128)(2,1)S(1)} %get-tuple-element.76), channel_id=1, source_target_pairs={{0,1},{1,0},{2,3},{3,2},{4,5},{5,4},{6,7},{7,6},{8,9},{9,8},{10,11... | collective-permute-start | bytes 589832 | tf_op jit(solution)/shard_map/ppermute | solution.py:146
  137.8 7.8 %collective-permute-start.24 = (bf16[32,3072]{1,0:T(8,128)(2,1)S(1)}, bf16[32,3072]{1,0:T(8,128)(2,1)S(1)}, u32[]{:S(2)}, u32[]{:S(2)}) collective-permute-start(bf16[32,3072]{1,0:T(8,128)(2,1)S(1)} %add_convert_fusion.9), channel_id=1, source_target_pairs={{0,3},{1,2},{2,1},{3,0},{4,7},{5,6},{6,5},{7,4},{8,11},{9,10},{10,... | collective-permute-start | bytes 589832 | tf_op jit(solution)/shard_map/ppermute | solution.py:146
  141.8 7.5 %collective-permute-start.27 = (bf16[32,3072]{1,0:T(8,128)(2,1)S(1)}, bf16[32,3072]{1,0:T(8,128)(2,1)S(1)}, u32[]{:S(2)}, u32[]{:S(2)}) collective-permute-start(bf16[32,3072]{1,0:T(8,128)(2,1)S(1)} %add_convert_fusion.7), channel_id=1, source_target_pairs={{0,3},{1,2},{2,1},{3,0},{4,7},{5,6},{6,5},{7,4},{8,11},{9,10},{10,... | collective-permute-start | bytes 589832 | tf_op jit(solution)/shard_map/ppermute | solution.py:146
  145.6 8.0 %collective-permute-start.29 = (bf16[32,3072]{1,0:T(8,128)(2,1)S(1)}, bf16[32,3072]{1,0:T(8,128)(2,1)S(1)}, u32[]{:S(2)}, u32[]{:S(2)}) collective-permute-start(bf16[32,3072]{1,0:T(8,128)(2,1)S(1)} %add_convert_fusion.8), channel_id=1, source_target_pairs={{0,5},{1,4},{2,7},{3,6},{4,9},{5,8},{6,11},{7,10},{8,13},{9,12},{1... | collective-permute-start | bytes 589832 | tf_op jit(solution)/shard_map/ppermute | solution.py:146
  145.7 8.0 %collective-permute-start.25 = (bf16[32,3072]{1,0:T(8,128)(2,1)S(1)}, bf16[32,3072]{1,0:T(8,128)(2,1)S(1)}, u32[]{:S(2)}, u32[]{:S(2)}) collective-permute-start(bf16[32,3072]{1,0:T(8,128)(2,1)S(1)} %add_convert_fusion.8), channel_id=1, source_target_pairs={{0,4},{1,5},{2,6},{3,7},{4,8},{5,9},{6,10},{7,11},{8,12},{9,13},{1... | collective-permute-start | bytes 589832 | tf_op jit(solution)/shard_map/ppermute | solution.py:146
  149.4 8.5 %collective-permute-start.28 = (bf16[32,3072]{1,0:T(8,128)(2,1)S(1)}, bf16[32,3072]{1,0:T(8,128)(2,1)S(1)}, u32[]{:S(2)}, u32[]{:S(2)}) collective-permute-start(bf16[32,3072]{1,0:T(8,128)(2,1)S(1)} %add_convert_fusion.6), channel_id=1, source_target_pairs={{0,4},{1,5},{2,6},{3,7},{4,8},{5,9},{6,10},{7,11},{8,12},{9,13},{1... | collective-permute-start | bytes 589832 | tf_op jit(solution)/shard_map/ppermute | solution.py:146
  160.9 7.6 %collective-permute-start.31 = (bf16[32,3072]{1,0:T(8,128)(2,1)S(1)}, bf16[32,3072]{1,0:T(8,128)(2,1)S(1)}, u32[]{:S(2)}, u32[]{:S(2)}) collective-permute-start(bf16[32,3072]{1,0:T(8,128)(2,1)S(1)} %get-tuple-element.83), channel_id=1, source_target_pairs={{0,1},{1,0},{2,3},{3,2},{4,5},{5,4},{6,7},{7,6},{8,9},{9,8},{10,11... | collective-permute-start | bytes 589832 | tf_op jit(solution)/shard_map/ppermute | solution.py:146
  171.1 9.9 %collective-permute-start.32 = (bf16[32,3072]{1,0:T(8,128)(2,1)S(1)}, bf16[32,3072]{1,0:T(8,128)(2,1)S(1)}, u32[]{:S(2)}, u32[]{:S(2)}) collective-permute-start(bf16[32,3072]{1,0:T(8,128)(2,1)S(1)} %add_convert_fusion.5), channel_id=1, source_target_pairs={{0,3},{1,2},{2,1},{3,0},{4,7},{5,6},{6,5},{7,4},{8,11},{9,10},{10,... | collective-permute-start | bytes 589832 | tf_op jit(solution)/shard_map/ppermute | solution.py:146
  174.8 9.2 %collective-permute-start.34 = (bf16[32,3072]{1,0:T(8,128)(2,1)S(1)}, bf16[32,3072]{1,0:T(8,128)(2,1)S(1)}, u32[]{:S(2)}, u32[]{:S(2)}) collective-permute-start(bf16[32,3072]{1,0:T(8,128)(2,1)S(1)} %add_convert_fusion.3), channel_id=1, source_target_pairs={{0,3},{1,2},{2,1},{3,0},{4,7},{5,6},{6,5},{7,4},{8,11},{9,10},{10,... | collective-permute-start | bytes 589832 | tf_op jit(solution)/shard_map/ppermute | solution.py:146
  181.1 8.5 %collective-permute-start.35 = (bf16[32,3072]{1,0:T(8,128)(2,1)S(1)}, bf16[32,3072]{1,0:T(8,128)(2,1)S(1)}, u32[]{:S(2)}, u32[]{:S(2)}) collective-permute-start(bf16[32,3072]{1,0:T(8,128)(2,1)S(1)} %add_convert_fusion.4.refs_0_), channel_id=1, source_target_pairs={{0,1},{1,0},{2,3},{3,2},{4,5},{5,4},{6,7},{7,6},{8,9},{9,8},{10,11... | collective-permute-start | bytes 589832 | tf_op jit(solution)/shard_map/ppermute | solution.py:146
  184.1 7.7 %collective-permute-start.36 = (bf16[32,3072]{1,0:T(8,128)(2,1)S(1)}, bf16[32,3072]{1,0:T(8,128)(2,1)S(1)}, u32[]{:S(2)}, u32[]{:S(2)}) collective-permute-start(bf16[32,3072]{1,0:T(8,128)(2,1)S(1)} %add_convert_fusion.2.refs_1_), channel_id=1, source_target_pairs={{0,1},{1,0},{2,3},{3,2},{4,5},{5,4},{6,7},{7,6},{8,9},{9,8},{10,11... | collective-permute-start | bytes 589832 | tf_op jit(solution)/shard_map/ppermute | solution.py:146
  195.1 7.5 %collective-permute-start.38 = (bf16[32,3072]{1,0:T(8,128)(2,1)S(1)}, bf16[32,3072]{1,0:T(8,128)(2,1)S(1)}, u32[]{:S(2)}, u32[]{:S(2)}) collective-permute-start(bf16[32,3072]{1,0:T(8,128)(2,1)S(1)} %get-tuple-element.93), channel_id=1, source_target_pairs={{0,5},{1,4},{2,7},{3,6},{4,9},{5,8},{6,11},{7,10},{8,13},{9,12},{1... | collective-permute-start | bytes 589832 | tf_op jit(solution)/shard_map/ppermute | solution.py:146
  195.1 14.4 %collective-permute-start.40 = (bf16[32,3072]{1,0:T(8,128)(2,1)S(1)}, bf16[32,3072]{1,0:T(8,128)(2,1)S(1)}, u32[]{:S(2)}, u32[]{:S(2)}) collective-permute-start(bf16[32,3072]{1,0:T(8,128)(2,1)S(1)} %get-tuple-element.94), channel_id=1, source_target_pairs={{0,6},{1,7},{2,4},{3,5},{4,10},{5,11},{6,8},{7,9},{8,14},{9,15},{1... | collective-permute-start | bytes 589832 | tf_op jit(solution)/shard_map/ppermute | solution.py:146
  195.8 21.9 %collective-permute-start.39 = (bf16[32,3072]{1,0:T(8,128)(2,1)S(1)}, bf16[32,3072]{1,0:T(8,128)(2,1)S(1)}, u32[]{:S(2)}, u32[]{:S(2)}) collective-permute-start(bf16[32,3072]{1,0:T(8,128)(2,1)S(1)} %broadcast_select_fusion), channel_id=1, source_target_pairs={{0,7},{1,6},{2,5},{3,4},{4,11},{5,10},{6,9},{7,8},{8,15},{9,14},{1... | collective-permute-start | bytes 589832 | tf_op jit(solution)/shard_map/ppermute | solution.py:146
  195.8 21.9 %collective-permute-start.37 = (bf16[32,3072]{1,0:T(8,128)(2,1)S(1)}, bf16[32,3072]{1,0:T(8,128)(2,1)S(1)}, u32[]{:S(2)}, u32[]{:S(2)}) collective-permute-start(bf16[32,3072]{1,0:T(8,128)(2,1)S(1)} %add_convert_fusion.1), channel_id=1, source_target_pairs={{0,4},{1,5},{2,6},{3,7},{4,8},{5,9},{6,10},{7,11},{8,12},{9,13},{1... | collective-permute-start | bytes 589832 | tf_op jit(solution)/shard_map/ppermute | solution.py:146
  (10 other events, 67.3 us)
where the time goes:
time: 217 us; the launch traced here: 218 us
  waiting for transfers between devices  126 us (58%)
  starting transfers between devices  62.7 us (29%)
  Pallas kernels  22.4 us (10%)
  between operations  2.79 us (1%)
  other arithmetic  2.71 us (1%)
    ppermute x41, waiting for transfers between devices, send(): return lax.ppermute(block, ('section', 'uly'), route)  126 us
    ppermute x41, starting transfers between devices, send(): return lax.ppermute(block, ('section', 'uly'), route)  62.7 us
    pallas_call x6, Pallas kernels, block_terms(): pl.pallas_call(functools.partial(block_kernel, count, len(rows_out)), out...  18.5 us
  transfers between devices with their start and end apart: 41, of which 37 were waited for; matrix products, arithmetic and copies ran while one was open for 1% of the time, Pallas kernels for 2%

commit v1 on v0

--- a/solution.py
+++ b/solution.py
@@ -206,7 +206,10 @@
     far = send(jnp.where(low, second, first), FAR, 1)
     near = send(jnp.where(low, near_first, near_second), NEAR, 1)
     base = send(rounded(before, jnp.where(low, first, second)), STAY, 1)
-    return rounded(base, near, far, cross)
+    total = lax.optimization_barrier(summed(cross))
+    for block in (far, near):
+        total = lax.optimization_barrier(total + block.astype(jnp.float32))
+    return (total + base.astype(jnp.float32)).astype(jnp.bfloat16)
 
 
 def shards(

time: 217 us -> 222 us (1.023)
  the two profiles are of different devices: /device:TPU:14 before, /device:TPU:0 now
where the time goes in v1:
time: 222 us
  waiting for transfers between devices  107 us (48%)
  starting transfers between devices  85.5 us (39%)
  Pallas kernels  22.4 us (10%)
  between operations  2.82 us (1%)
  other arithmetic  2.75 us (1%)
    ppermute x41, waiting for transfers between devices, send(): return lax.ppermute(block, ('section', 'uly'), route)  107 us
    ppermute x41, starting transfers between devices, send(): return lax.ppermute(block, ('section', 'uly'), route)  85.5 us
    pallas_call x6, Pallas kernels, block_terms(): pl.pallas_call(functools.partial(block_kernel, count, len(rows_out)), out...  18.5 us
  transfers between devices with their start and end apart: 41, of which 30 were waited for; matrix products, arithmetic and copies ran while one was open for 1% of the time, Pallas kernels for 2%

profile of v1, /device:TPU:0, one launch (start us, length us, event | category | flops | bytes accessed | tf_op | source)
XLA Modules:
  0.0 222.3 jit_solution(14432589577197745755)
XLA Ops:
  0.0 5.0 %collective-permute-start = (bf16[32,3072]{1,0:T(8,128)(2,1)}, bf16[32,3072]{1,0:T(8,128)(2,1)S(1)}, u32[]{:S(2)}, u32[]{:S(2)}) collective-permute-start(bf16[32,3072]{1,0:T(8,128)(2,1)} %bitcast.15), channel_id=1, source_target_pairs={{0,3},{1,2},{2,1},{3,0},{4,7},{5,6},{6,5},{7,4},{8,11},{9,10},{10,... | collective-permute-start | bytes 589832 | tf_op jit(solution)/shard_map/ppermute | solution.py:146
  7.8 3.9 %shard_map.82 = (bf16[3072,1152]{1,0:T(8,128)(2,1)S(1)}, bf16[384,3072]{1,0:T(8,128)(2,1)S(1)}, bf16[512,384]{1,0:T(8,128)(2,1)S(1)}, bf16[512,384]{1,0:T(8,128)(2,1)S(1)}, bf16[1,3072]{1,0:T(2,128)(2,1)S(1)}) custom-call(bf16[3,3072,384]{2,1,0:T(8,128)(2,1)} %bitcast.11, bf16[384,3072]{1,0:T(8,128)(2,1)} %bitcast.12, bf16[512,384]{1,0:T(8,128)(2,1)} %bitcast.13, ...), custom_call_target="tpu_custom_call" | custom-call | bytes 10229760 | tf_op jit(solution)/shard_map/pallas_call | solution.py:95
  14.6 4.1 %collective-permute-done.2 = bf16[32,3072]{1,0:T(8,128)(2,1)S(1)} collective-permute-done((bf16[32,3072]{1,0:T(8,128)(2,1)S(1)}, bf16[32,3072]{1,0:T(8,128)(2,1)S(1)}, u32[]{:S(2)}, u32[]{:S(2)}) %collective-permute-start.2) | collective-permute-done | bytes 196640 | tf_op jit(solution)/shard_map/ppermute | solution.py:146
  18.8 3.1 %shard_map.83 = (bf16[32,3072]{1,0:T(8,128)(2,1)S(1)}, bf16[32,3072]{1,0:T(8,128)(2,1)S(1)}, bf16[32,3072]{1,0:T(8,128)(2,1)S(1)}, bf16[32,3072]{1,0:T(8,128)(2,...) custom-call(s32[2]{0:T(128)S(1)} %pad_add_fusion.3.info, ...), custom_call_target="tpu_custom_call", output_to_operand_aliasing={{4}: (8, {}), {5}: (9, {})} | custom-call | flops 1308622848 | bytes 9437184 | tf_op jit(solution)/shard_map/pallas_call | solution.py:115
  23.5 4.2 %collective-permute-done.3 = bf16[32,3072]{1,0:T(8,128)(2,1)S(1)} collective-permute-done((bf16[32,3072]{1,0:T(8,128)(2,1)S(1)}, bf16[32,3072]{1,0:T(8,128)(2,1)S(1)}, u32[]{:S(2)}, u32[]{:S(2)}) %collective-permute-start.3) | collective-permute-done | bytes 196640 | tf_op jit(solution)/shard_map/ppermute | solution.py:146
  31.6 4.5 %collective-permute-done.5 = bf16[32,3072]{1,0:T(8,128)(2,1)S(1)} collective-permute-done((bf16[32,3072]{1,0:T(8,128)(2,1)S(1)}, bf16[32,3072]{1,0:T(8,128)(2,1)S(1)}, u32[]{:S(2)}, u32[]{:S(2)}) %collective-permute-start.5) | collective-permute-done | bytes 196640 | tf_op jit(solution)/shard_map/ppermute | solution.py:146
  36.2 4.4 %collective-permute-start.6 = (bf16[32,3072]{1,0:T(8,128)(2,1)S(1)}, bf16[32,3072]{1,0:T(8,128)(2,1)S(1)}, u32[]{:S(2)}, u32[]{:S(2)}) collective-permute-start(bf16[32,3072]{1,0:T(8,128)(2,1)S(1)} %add_convert_fusion.19), channel_id=1, source_target_pairs={{0,3},{1,2},{2,1},{3,0},{4,7},{5,6},{6,5},{7,4},{8,11},{9,10},{10,... | collective-permute-start | bytes 589832 | tf_op jit(solution)/shard_map/ppermute | solution.py:146
  47.3 3.6 %collective-permute-done.8.refs_3_ = bf16[32,3072]{1,0:T(8,128)(2,1)S(1)} collective-permute-done((bf16[32,3072]{1,0:T(8,128)(2,1)S(1)}, bf16[32,3072]{1,0:T(8,128)(2,1)S(1)}, u32[]{:S(2)}, u32[]{:S(2)}) %collective-permute-start.8) | collective-permute-done | bytes 196640 | tf_op jit(solution)/shard_map/ppermute | solution.py:146
  50.8 3.1 %shard_map.84 = (bf16[32,3072]{1,0:T(8,128)(2,1)S(1)}, bf16[32,3072]{1,0:T(8,128)(2,1)S(1)}, bf16[32,3072]{1,0:T(8,128)(2,1)S(1)}, bf16[32,3072]{1,0:T(8,128)(2,...) custom-call(s32[2]{0:T(128)S(1)} %pad_add_fusion.2.info, ...), custom_call_target="tpu_custom_call", output_to_operand_aliasing={{4}: (8, {}), {5}: (9, {})} | custom-call | flops 1308622848 | bytes 9437184 | tf_op jit(solution)/shard_map/pallas_call | solution.py:115
  56.0 5.3 %collective-permute-done.9 = bf16[32,3072]{1,0:T(8,128)(2,1)S(1)} collective-permute-done((bf16[32,3072]{1,0:T(8,128)(2,1)S(1)}, bf16[32,3072]{1,0:T(8,128)(2,1)S(1)}, u32[]{:S(2)}, u32[]{:S(2)}) %collective-permute-start.9) | collective-permute-done | bytes 196640 | tf_op jit(solution)/shard_map/ppermute | solution.py:146
  69.8 6.5 %collective-permute-start.13 = (bf16[32,3072]{1,0:T(8,128)(2,1)S(1)}, bf16[32,3072]{1,0:T(8,128)(2,1)S(1)}, u32[]{:S(2)}, u32[]{:S(2)}) collective-permute-start(bf16[32,3072]{1,0:T(8,128)(2,1)S(1)} %add_convert_fusion.15), channel_id=1, source_target_pairs={{0,3},{1,2},{2,1},{3,0},{4,7},{5,6},{6,5},{7,4},{8,11},{9,10},{10,... | collective-permute-start | bytes 589832 | tf_op jit(solution)/shard_map/ppermute | solution.py:146
  76.4 4.2 %collective-permute-done.13 = bf16[32,3072]{1,0:T(8,128)(2,1)S(1)} collective-permute-done((bf16[32,3072]{1,0:T(8,128)(2,1)S(1)}, bf16[32,3072]{1,0:T(8,128)(2,1)S(1)}, u32[]{:S(2)}, u32[]{:S(2)}) %collective-permute-start.13) | collective-permute-done | bytes 196640 | tf_op jit(solution)/shard_map/ppermute | solution.py:146
  84.5 4.0 %collective-permute-done.16.refs_3_ = bf16[32,3072]{1,0:T(8,128)(2,1)S(1)} collective-permute-done((bf16[32,3072]{1,0:T(8,128)(2,1)S(1)}, bf16[32,3072]{1,0:T(8,128)(2,1)S(1)}, u32[]{:S(2)}, u32[]{:S(2)}) %collective-permute-start.16) | collective-permute-done | bytes 196640 | tf_op jit(solution)/shard_map/ppermute | solution.py:146
  89.0 3.0 %shard_map.85 = (bf16[32,3072]{1,0:T(8,128)(2,1)S(1)}, bf16[32,3072]{1,0:T(8,128)(2,1)S(1)}, bf16[32,3072]{1,0:T(8,128)(2,1)S(1)}, bf16[32,3072]{1,0:T(8,128)(2,...) custom-call(s32[2]{0:T(128)S(1)} %pad_add_fusion.5.info, ...), custom_call_target="tpu_custom_call", output_to_operand_aliasing={{4}: (8, {}), {5}: (9, {})} | custom-call | flops 1308622848 | bytes 9437184 | tf_op jit(solution)/shard_map/pallas_call | solution.py:115
  92.9 4.9 %collective-permute-done.17 = bf16[32,3072]{1,0:T(8,128)(2,1)S(1)} collective-permute-done((bf16[32,3072]{1,0:T(8,128)(2,1)S(1)}, bf16[32,3072]{1,0:T(8,128)(2,1)S(1)}, u32[]{:S(2)}, u32[]{:S(2)}) %collective-permute-start.17) | collective-permute-done | bytes 196640 | tf_op jit(solution)/shard_map/ppermute | solution.py:146
  102.3 3.3 %collective-permute-done.19 = bf16[32,3072]{1,0:T(8,128)(2,1)S(1)} collective-permute-done((bf16[32,3072]{1,0:T(8,128)(2,1)S(1)}, bf16[32,3072]{1,0:T(8,128)(2,1)S(1)}, u32[]{:S(2)}, u32[]{:S(2)}) %collective-permute-start.19) | collective-permute-done | bytes 196640 | tf_op jit(solution)/shard_map/ppermute | solution.py:146
  105.6 8.5 %collective-permute-start.20 = (bf16[32,3072]{1,0:T(8,128)(2,1)S(1)}, bf16[32,3072]{1,0:T(8,128)(2,1)S(1)}, u32[]{:S(2)}, u32[]{:S(2)}) collective-permute-start(bf16[32,3072]{1,0:T(8,128)(2,1)S(1)} %add_convert_fusion.11), channel_id=1, source_target_pairs={{0,3},{1,2},{2,1},{3,0},{4,7},{5,6},{6,5},{7,4},{8,11},{9,10},{10,... | collective-permute-start | bytes 589832 | tf_op jit(solution)/shard_map/ppermute | solution.py:146
  114.2 4.2 %collective-permute-done.20 = bf16[32,3072]{1,0:T(8,128)(2,1)S(1)} collective-permute-done((bf16[32,3072]{1,0:T(8,128)(2,1)S(1)}, bf16[32,3072]{1,0:T(8,128)(2,1)S(1)}, u32[]{:S(2)}, u32[]{:S(2)}) %collective-permute-start.20) | collective-permute-done | bytes 196640 | tf_op jit(solution)/shard_map/ppermute | solution.py:146
  121.2 3.3 %collective-permute-done.22.refs_3_ = bf16[32,3072]{1,0:T(8,128)(2,1)S(1)} collective-permute-done((bf16[32,3072]{1,0:T(8,128)(2,1)S(1)}, bf16[32,3072]{1,0:T(8,128)(2,1)S(1)}, u32[]{:S(2)}, u32[]{:S(2)}) %collective-permute-start.22) | collective-permute-done | bytes 196640 | tf_op jit(solution)/shard_map/ppermute | solution.py:146
  124.5 3.2 %shard_map.86 = (bf16[32,3072]{1,0:T(8,128)(2,1)S(1)}, bf16[32,3072]{1,0:T(8,128)(2,1)S(1)}, bf16[32,3072]{1,0:T(8,128)(2,1)S(1)}, bf16[32,3072]{1,0:T(8,128)(2,...) custom-call(s32[2]{0:T(128)S(1)} %pad_add_fusion.4.info, ...), custom_call_target="tpu_custom_call", output_to_operand_aliasing={{4}: (8, {}), {5}: (9, {})} | custom-call | flops 1308622848 | bytes 9437184 | tf_op jit(solution)/shard_map/pallas_call | solution.py:115
  129.3 4.8 %collective-permute-done.23 = bf16[32,3072]{1,0:T(8,128)(2,1)S(1)} collective-permute-done((bf16[32,3072]{1,0:T(8,128)(2,1)S(1)}, bf16[32,3072]{1,0:T(8,128)(2,1)S(1)}, u32[]{:S(2)}, u32[]{:S(2)}) %collective-permute-start.23) | collective-permute-done | bytes 196640 | tf_op jit(solution)/shard_map/ppermute | solution.py:146
  136.7 6.1 %collective-permute-start.24 = (bf16[32,3072]{1,0:T(8,128)(2,1)S(1)}, bf16[32,3072]{1,0:T(8,128)(2,1)S(1)}, u32[]{:S(2)}, u32[]{:S(2)}) collective-permute-start(bf16[32,3072]{1,0:T(8,128)(2,1)S(1)} %add_convert_fusion.9), channel_id=1, source_target_pairs={{0,3},{1,2},{2,1},{3,0},{4,7},{5,6},{6,5},{7,4},{8,11},{9,10},{10,... | collective-permute-start | bytes 589832 | tf_op jit(solution)/shard_map/ppermute | solution.py:146
  142.9 7.8 %collective-permute-start.27 = (bf16[32,3072]{1,0:T(8,128)(2,1)S(1)}, bf16[32,3072]{1,0:T(8,128)(2,1)S(1)}, u32[]{:S(2)}, u32[]{:S(2)}) collective-permute-start(bf16[32,3072]{1,0:T(8,128)(2,1)S(1)} %add_convert_fusion.7), channel_id=1, source_target_pairs={{0,3},{1,2},{2,1},{3,0},{4,7},{5,6},{6,5},{7,4},{8,11},{9,10},{10,... | collective-permute-start | bytes 589832 | tf_op jit(solution)/shard_map/ppermute | solution.py:146
  151.5 4.2 %collective-permute-done.27 = bf16[32,3072]{1,0:T(8,128)(2,1)S(1)} collective-permute-done((bf16[32,3072]{1,0:T(8,128)(2,1)S(1)}, bf16[32,3072]{1,0:T(8,128)(2,1)S(1)}, u32[]{:S(2)}, u32[]{:S(2)}) %collective-permute-start.27) | collective-permute-done | bytes 196640 | tf_op jit(solution)/shard_map/ppermute | solution.py:146
  156.6 3.3 %collective-permute-done.29.refs_2_ = bf16[32,3072]{1,0:T(8,128)(2,1)S(1)} collective-permute-done((bf16[32,3072]{1,0:T(8,128)(2,1)S(1)}, bf16[32,3072]{1,0:T(8,128)(2,1)S(1)}, u32[]{:S(2)}, u32[]{:S(2)}) %collective-permute-start.29) | collective-permute-done | bytes 196640 | tf_op jit(solution)/shard_map/ppermute | solution.py:146
  164.0 3.0 %shard_map.87 = (bf16[32,3072]{1,0:T(8,128)(2,1)S(1)}, bf16[32,3072]{1,0:T(8,128)(2,1)S(1)}, bf16[32,3072]{1,0:T(8,128)(2,1)S(1)}, bf16[32,3072]{1,0:T(8,128)(2,...) custom-call(s32[2]{0:T(128)S(1)} %pad_add_fusion.info, ...), custom_call_target="tpu_custom_call", output_to_operand_aliasing={{4}: (8, {}), {5}: (9, {})} | custom-call | flops 1308622848 | bytes 9437184 | tf_op jit(solution)/shard_map/pallas_call | solution.py:115
  167.4 5.9 %collective-permute-done.31 = bf16[32,3072]{1,0:T(8,128)(2,1)S(1)} collective-permute-done((bf16[32,3072]{1,0:T(8,128)(2,1)S(1)}, bf16[32,3072]{1,0:T(8,128)(2,1)S(1)}, u32[]{:S(2)}, u32[]{:S(2)}) %collective-permute-start.31) | collective-permute-done | bytes 196640 | tf_op jit(solution)/shard_map/ppermute | solution.py:146
  174.6 3.7 %collective-permute-start.32 = (bf16[32,3072]{1,0:T(8,128)(2,1)S(1)}, bf16[32,3072]{1,0:T(8,128)(2,1)S(1)}, u32[]{:S(2)}, u32[]{:S(2)}) collective-permute-start(bf16[32,3072]{1,0:T(8,128)(2,1)S(1)} %add_convert_fusion.5), channel_id=1, source_target_pairs={{0,3},{1,2},{2,1},{3,0},{4,7},{5,6},{6,5},{7,4},{8,11},{9,10},{10,... | collective-permute-start | bytes 589832 | tf_op jit(solution)/shard_map/ppermute | solution.py:146
  181.3 9.3 %collective-permute-start.34 = (bf16[32,3072]{1,0:T(8,128)(2,1)S(1)}, bf16[32,3072]{1,0:T(8,128)(2,1)S(1)}, u32[]{:S(2)}, u32[]{:S(2)}) collective-permute-start(bf16[32,3072]{1,0:T(8,128)(2,1)S(1)} %add_convert_fusion.3), channel_id=1, source_target_pairs={{0,3},{1,2},{2,1},{3,0},{4,7},{5,6},{6,5},{7,4},{8,11},{9,10},{10,... | collective-permute-start | bytes 589832 | tf_op jit(solution)/shard_map/ppermute | solution.py:146
  190.7 4.4 %collective-permute-done.34 = bf16[32,3072]{1,0:T(8,128)(2,1)S(1)} collective-permute-done((bf16[32,3072]{1,0:T(8,128)(2,1)S(1)}, bf16[32,3072]{1,0:T(8,128)(2,1)S(1)}, u32[]{:S(2)}, u32[]{:S(2)}) %collective-permute-start.34) | collective-permute-done | bytes 196640 | tf_op jit(solution)/shard_map/ppermute | solution.py:146
  196.8 4.1 %collective-permute-done.36.refs_3_ = bf16[32,3072]{1,0:T(8,128)(2,1)S(1)} collective-permute-done((bf16[32,3072]{1,0:T(8,128)(2,1)S(1)}, bf16[32,3072]{1,0:T(8,128)(2,1)S(1)}, u32[]{:S(2)}, u32[]{:S(2)}) %collective-permute-start.36) | collective-permute-done | bytes 196640 | tf_op jit(solution)/shard_map/ppermute | solution.py:146
  206.0 13.9 %collective-permute-done.37 = bf16[32,3072]{1,0:T(8,128)(2,1)S(1)} collective-permute-done((bf16[32,3072]{1,0:T(8,128)(2,1)S(1)}, bf16[32,3072]{1,0:T(8,128)(2,1)S(1)}, u32[]{:S(2)}, u32[]{:S(2)}) %collective-permute-start.37) | collective-permute-done | bytes 196640 | tf_op jit(solution)/shard_map/ppermute | solution.py:146
  (95 shorter events, 62.9 us)
Async XLA Ops:
  0.0 11.8 %collective-permute-start = (bf16[32,3072]{1,0:T(8,128)(2,1)}, bf16[32,3072]{1,0:T(8,128)(2,1)S(1)}, u32[]{:S(2)}, u32[]{:S(2)}) collective-permute-start(bf16[32,3072]{1,0:T(8,128)(2,1)} %bitcast.15), channel_id=1, source_target_pairs={{0,3},{1,2},{2,1},{3,0},{4,7},{5,6},{6,5},{7,4},{8,11},{9,10},{10,... | collective-permute-start | bytes 589832 | tf_op jit(solution)/shard_map/ppermute | solution.py:146
  5.1 9.6 %collective-permute-start.1 = (bf16[32,3072]{1,0:T(8,128)(2,1)}, bf16[32,3072]{1,0:T(8,128)(2,1)S(1)}, u32[]{:S(2)}, u32[]{:S(2)}) collective-permute-start(bf16[32,3072]{1,0:T(8,128)(2,1)} %bitcast.16), channel_id=1, source_target_pairs={{0,1},{1,0},{2,3},{3,2},{4,5},{5,4},{6,7},{7,6},{8,9},{9,8},{10,11... | collective-permute-start | bytes 589832 | tf_op jit(solution)/shard_map/ppermute | solution.py:146
  11.8 6.9 %collective-permute-start.2 = (bf16[32,3072]{1,0:T(8,128)(2,1)S(1)}, bf16[32,3072]{1,0:T(8,128)(2,1)S(1)}, u32[]{:S(2)}, u32[]{:S(2)}) collective-permute-start(bf16[32,3072]{1,0:T(8,128)(2,1)S(1)} %collective-permute-done), channel_id=1, source_target_pairs={{0,1},{1,0},{2,3},{3,2},{4,5},{5,4},{6,7},{7,6},{8,9},{9,8},{10,11... | collective-permute-start | bytes 589832 | tf_op jit(solution)/shard_map/ppermute | solution.py:146
  27.7 8.4 %collective-permute-start.5 = (bf16[32,3072]{1,0:T(8,128)(2,1)S(1)}, bf16[32,3072]{1,0:T(8,128)(2,1)S(1)}, u32[]{:S(2)}, u32[]{:S(2)}) collective-permute-start(bf16[32,3072]{1,0:T(8,128)(2,1)S(1)} %get-tuple-element.58), channel_id=1, source_target_pairs={{0,1},{1,0},{2,3},{3,2},{4,5},{5,4},{6,7},{7,6},{8,9},{9,8},{10,11... | collective-permute-start | bytes 589832 | tf_op jit(solution)/shard_map/ppermute | solution.py:146
  29.3 11.2 %collective-permute-start.4 = (bf16[32,3072]{1,0:T(8,128)(2,1)S(1)}, bf16[32,3072]{1,0:T(8,128)(2,1)S(1)}, u32[]{:S(2)}, u32[]{:S(2)}) collective-permute-start(bf16[32,3072]{1,0:T(8,128)(2,1)S(1)} %add_convert_fusion.21), channel_id=1, source_target_pairs={{0,3},{1,2},{2,1},{3,0},{4,7},{5,6},{6,5},{7,4},{8,11},{9,10},{10,... | collective-permute-start | bytes 589832 | tf_op jit(solution)/shard_map/ppermute | solution.py:146
  36.2 8.1 %collective-permute-start.6 = (bf16[32,3072]{1,0:T(8,128)(2,1)S(1)}, bf16[32,3072]{1,0:T(8,128)(2,1)S(1)}, u32[]{:S(2)}, u32[]{:S(2)}) collective-permute-start(bf16[32,3072]{1,0:T(8,128)(2,1)S(1)} %add_convert_fusion.19), channel_id=1, source_target_pairs={{0,3},{1,2},{2,1},{3,0},{4,7},{5,6},{6,5},{7,4},{8,11},{9,10},{10,... | collective-permute-start | bytes 589832 | tf_op jit(solution)/shard_map/ppermute | solution.py:146
  53.9 7.5 %collective-permute-start.9 = (bf16[32,3072]{1,0:T(8,128)(2,1)S(1)}, bf16[32,3072]{1,0:T(8,128)(2,1)S(1)}, u32[]{:S(2)}, u32[]{:S(2)}) collective-permute-start(bf16[32,3072]{1,0:T(8,128)(2,1)S(1)} %get-tuple-element.62), channel_id=1, source_target_pairs={{0,1},{1,0},{2,3},{3,2},{4,5},{5,4},{6,7},{7,6},{8,9},{9,8},{10,11... | collective-permute-start | bytes 589832 | tf_op jit(solution)/shard_map/ppermute | solution.py:146
  61.4 8.3 %collective-permute-start.12 = (bf16[32,3072]{1,0:T(8,128)(2,1)S(1)}, bf16[32,3072]{1,0:T(8,128)(2,1)S(1)}, u32[]{:S(2)}, u32[]{:S(2)}) collective-permute-start(bf16[32,3072]{1,0:T(8,128)(2,1)S(1)} %get-tuple-element.65), channel_id=1, source_target_pairs={{0,1},{1,0},{2,3},{3,2},{4,5},{5,4},{6,7},{7,6},{8,9},{9,8},{10,11... | collective-permute-start | bytes 589832 | tf_op jit(solution)/shard_map/ppermute | solution.py:146
  63.9 12.3 %collective-permute-start.10 = (bf16[32,3072]{1,0:T(8,128)(2,1)S(1)}, bf16[32,3072]{1,0:T(8,128)(2,1)S(1)}, u32[]{:S(2)}, u32[]{:S(2)}) collective-permute-start(bf16[32,3072]{1,0:T(8,128)(2,1)S(1)} %add_convert_fusion.17), channel_id=1, source_target_pairs={{0,3},{1,2},{2,1},{3,0},{4,7},{5,6},{6,5},{7,4},{8,11},{9,10},{10,... | collective-permute-start | bytes 589832 | tf_op jit(solution)/shard_map/ppermute | solution.py:146
  69.8 10.9 %collective-permute-start.13 = (bf16[32,3072]{1,0:T(8,128)(2,1)S(1)}, bf16[32,3072]{1,0:T(8,128)(2,1)S(1)}, u32[]{:S(2)}, u32[]{:S(2)}) collective-permute-start(bf16[32,3072]{1,0:T(8,128)(2,1)S(1)} %add_convert_fusion.15), channel_id=1, source_target_pairs={{0,3},{1,2},{2,1},{3,0},{4,7},{5,6},{6,5},{7,4},{8,11},{9,10},{10,... | collective-permute-start | bytes 589832 | tf_op jit(solution)/shard_map/ppermute | solution.py:146
  76.3 7.9 %collective-permute-start.15 = (bf16[32,3072]{1,0:T(8,128)(2,1)S(1)}, bf16[32,3072]{1,0:T(8,128)(2,1)S(1)}, u32[]{:S(2)}, u32[]{:S(2)}) collective-permute-start(bf16[32,3072]{1,0:T(8,128)(2,1)S(1)} %add_convert_fusion.16), channel_id=1, source_target_pairs={{0,5},{1,4},{2,7},{3,6},{4,9},{5,8},{6,11},{7,10},{8,13},{9,12},{1... | collective-permute-start | bytes 589832 | tf_op jit(solution)/shard_map/ppermute | solution.py:146
  76.4 8.2 %collective-permute-start.11 = (bf16[32,3072]{1,0:T(8,128)(2,1)S(1)}, bf16[32,3072]{1,0:T(8,128)(2,1)S(1)}, u32[]{:S(2)}, u32[]{:S(2)}) collective-permute-start(bf16[32,3072]{1,0:T(8,128)(2,1)S(1)} %add_convert_fusion.16), channel_id=1, source_target_pairs={{0,4},{1,5},{2,6},{3,7},{4,8},{5,9},{6,10},{7,11},{8,12},{9,13},{1... | collective-permute-start | bytes 589832 | tf_op jit(solution)/shard_map/ppermute | solution.py:146
  80.8 7.7 %collective-permute-start.16 = (bf16[32,3072]{1,0:T(8,128)(2,1)S(1)}, bf16[32,3072]{1,0:T(8,128)(2,1)S(1)}, u32[]{:S(2)}, u32[]{:S(2)}) collective-permute-start(bf16[32,3072]{1,0:T(8,128)(2,1)S(1)} %add_convert_fusion.14), channel_id=1, source_target_pairs={{0,5},{1,4},{2,7},{3,6},{4,9},{5,8},{6,11},{7,10},{8,13},{9,12},{1... | collective-permute-start | bytes 589832 | tf_op jit(solution)/shard_map/ppermute | solution.py:146
  80.8 8.2 %collective-permute-start.14 = (bf16[32,3072]{1,0:T(8,128)(2,1)S(1)}, bf16[32,3072]{1,0:T(8,128)(2,1)S(1)}, u32[]{:S(2)}, u32[]{:S(2)}) collective-permute-start(bf16[32,3072]{1,0:T(8,128)(2,1)S(1)} %add_convert_fusion.14), channel_id=1, source_target_pairs={{0,4},{1,5},{2,6},{3,7},{4,8},{5,9},{6,10},{7,11},{8,12},{9,13},{1... | collective-permute-start | bytes 589832 | tf_op jit(solution)/shard_map/ppermute | solution.py:146
  97.8 7.7 %collective-permute-start.19 = (bf16[32,3072]{1,0:T(8,128)(2,1)S(1)}, bf16[32,3072]{1,0:T(8,128)(2,1)S(1)}, u32[]{:S(2)}, u32[]{:S(2)}) collective-permute-start(bf16[32,3072]{1,0:T(8,128)(2,1)S(1)} %get-tuple-element.72), channel_id=1, source_target_pairs={{0,1},{1,0},{2,3},{3,2},{4,5},{5,4},{6,7},{7,6},{8,9},{9,8},{10,11... | collective-permute-start | bytes 589832 | tf_op jit(solution)/shard_map/ppermute | solution.py:146
  99.6 14.4 %collective-permute-start.18 = (bf16[32,3072]{1,0:T(8,128)(2,1)S(1)}, bf16[32,3072]{1,0:T(8,128)(2,1)S(1)}, u32[]{:S(2)}, u32[]{:S(2)}) collective-permute-start(bf16[32,3072]{1,0:T(8,128)(2,1)S(1)} %add_convert_fusion.13), channel_id=1, source_target_pairs={{0,3},{1,2},{2,1},{3,0},{4,7},{5,6},{6,5},{7,4},{8,11},{9,10},{10,... | collective-permute-start | bytes 589832 | tf_op jit(solution)/shard_map/ppermute | solution.py:146
  105.6 12.8 %collective-permute-start.20 = (bf16[32,3072]{1,0:T(8,128)(2,1)S(1)}, bf16[32,3072]{1,0:T(8,128)(2,1)S(1)}, u32[]{:S(2)}, u32[]{:S(2)}) collective-permute-start(bf16[32,3072]{1,0:T(8,128)(2,1)S(1)} %add_convert_fusion.11), channel_id=1, source_target_pairs={{0,3},{1,2},{2,1},{3,0},{4,7},{5,6},{6,5},{7,4},{8,11},{9,10},{10,... | collective-permute-start | bytes 589832 | tf_op jit(solution)/shard_map/ppermute | solution.py:146
  114.1 7.1 %collective-permute-start.21 = (bf16[32,3072]{1,0:T(8,128)(2,1)S(1)}, bf16[32,3072]{1,0:T(8,128)(2,1)S(1)}, u32[]{:S(2)}, u32[]{:S(2)}) collective-permute-start(bf16[32,3072]{1,0:T(8,128)(2,1)S(1)} %add_convert_fusion.12.refs_0_), channel_id=1, source_target_pairs={{0,1},{1,0},{2,3},{3,2},{4,5},{5,4},{6,7},{7,6},{8,9},{9,8},{10,11... | collective-permute-start | bytes 589832 | tf_op jit(solution)/shard_map/ppermute | solution.py:146
  134.2 8.6 %collective-permute-start.26 = (bf16[32,3072]{1,0:T(8,128)(2,1)S(1)}, bf16[32,3072]{1,0:T(8,128)(2,1)S(1)}, u32[]{:S(2)}, u32[]{:S(2)}) collective-permute-start(bf16[32,3072]{1,0:T(8,128)(2,1)S(1)} %get-tuple-element.79), channel_id=1, source_target_pairs={{0,1},{1,0},{2,3},{3,2},{4,5},{5,4},{6,7},{7,6},{8,9},{9,8},{10,11... | collective-permute-start | bytes 589832 | tf_op jit(solution)/shard_map/ppermute | solution.py:146
  136.7 13.9 %collective-permute-start.24 = (bf16[32,3072]{1,0:T(8,128)(2,1)S(1)}, bf16[32,3072]{1,0:T(8,128)(2,1)S(1)}, u32[]{:S(2)}, u32[]{:S(2)}) collective-permute-start(bf16[32,3072]{1,0:T(8,128)(2,1)S(1)} %add_convert_fusion.9), channel_id=1, source_target_pairs={{0,3},{1,2},{2,1},{3,0},{4,7},{5,6},{6,5},{7,4},{8,11},{9,10},{10,... | collective-permute-start | bytes 589832 | tf_op jit(solution)/shard_map/ppermute | solution.py:146
  142.9 12.9 %collective-permute-start.27 = (bf16[32,3072]{1,0:T(8,128)(2,1)S(1)}, bf16[32,3072]{1,0:T(8,128)(2,1)S(1)}, u32[]{:S(2)}, u32[]{:S(2)}) collective-permute-start(bf16[32,3072]{1,0:T(8,128)(2,1)S(1)} %add_convert_fusion.7), channel_id=1, source_target_pairs={{0,3},{1,2},{2,1},{3,0},{4,7},{5,6},{6,5},{7,4},{8,11},{9,10},{10,... | collective-permute-start | bytes 589832 | tf_op jit(solution)/shard_map/ppermute | solution.py:146
  150.7 9.2 %collective-permute-start.29 = (bf16[32,3072]{1,0:T(8,128)(2,1)S(1)}, bf16[32,3072]{1,0:T(8,128)(2,1)S(1)}, u32[]{:S(2)}, u32[]{:S(2)}) collective-permute-start(bf16[32,3072]{1,0:T(8,128)(2,1)S(1)} %add_convert_fusion.8), channel_id=1, source_target_pairs={{0,5},{1,4},{2,7},{3,6},{4,9},{5,8},{6,11},{7,10},{8,13},{9,12},{1... | collective-permute-start | bytes 589832 | tf_op jit(solution)/shard_map/ppermute | solution.py:146
  150.8 9.2 %collective-permute-start.25 = (bf16[32,3072]{1,0:T(8,128)(2,1)S(1)}, bf16[32,3072]{1,0:T(8,128)(2,1)S(1)}, u32[]{:S(2)}, u32[]{:S(2)}) collective-permute-start(bf16[32,3072]{1,0:T(8,128)(2,1)S(1)} %add_convert_fusion.8), channel_id=1, source_target_pairs={{0,4},{1,5},{2,6},{3,7},{4,8},{5,9},{6,10},{7,11},{8,12},{9,13},{1... | collective-permute-start | bytes 589832 | tf_op jit(solution)/shard_map/ppermute | solution.py:146
  155.8 7.0 %collective-permute-start.30 = (bf16[32,3072]{1,0:T(8,128)(2,1)S(1)}, bf16[32,3072]{1,0:T(8,128)(2,1)S(1)}, u32[]{:S(2)}, u32[]{:S(2)}) collective-permute-start(bf16[32,3072]{1,0:T(8,128)(2,1)S(1)} %add_convert_fusion.6), channel_id=1, source_target_pairs={{0,5},{1,4},{2,7},{3,6},{4,9},{5,8},{6,11},{7,10},{8,13},{9,12},{1... | collective-permute-start | bytes 589832 | tf_op jit(solution)/shard_map/ppermute | solution.py:146
  155.9 8.2 %collective-permute-start.28 = (bf16[32,3072]{1,0:T(8,128)(2,1)S(1)}, bf16[32,3072]{1,0:T(8,128)(2,1)S(1)}, u32[]{:S(2)}, u32[]{:S(2)}) collective-permute-start(bf16[32,3072]{1,0:T(8,128)(2,1)S(1)} %add_convert_fusion.6), channel_id=1, source_target_pairs={{0,4},{1,5},{2,6},{3,7},{4,8},{5,9},{6,10},{7,11},{8,12},{9,13},{1... | collective-permute-start | bytes 589832 | tf_op jit(solution)/shard_map/ppermute | solution.py:146
  173.4 7.8 %collective-permute-start.33 = (bf16[32,3072]{1,0:T(8,128)(2,1)S(1)}, bf16[32,3072]{1,0:T(8,128)(2,1)S(1)}, u32[]{:S(2)}, u32[]{:S(2)}) collective-permute-start(bf16[32,3072]{1,0:T(8,128)(2,1)S(1)} %get-tuple-element.86), channel_id=1, source_target_pairs={{0,1},{1,0},{2,3},{3,2},{4,5},{5,4},{6,7},{7,6},{8,9},{9,8},{10,11... | collective-permute-start | bytes 589832 | tf_op jit(solution)/shard_map/ppermute | solution.py:146
  174.6 16.0 %collective-permute-start.32 = (bf16[32,3072]{1,0:T(8,128)(2,1)S(1)}, bf16[32,3072]{1,0:T(8,128)(2,1)S(1)}, u32[]{:S(2)}, u32[]{:S(2)}) collective-permute-start(bf16[32,3072]{1,0:T(8,128)(2,1)S(1)} %add_convert_fusion.5), channel_id=1, source_target_pairs={{0,3},{1,2},{2,1},{3,0},{4,7},{5,6},{6,5},{7,4},{8,11},{9,10},{10,... | collective-permute-start | bytes 589832 | tf_op jit(solution)/shard_map/ppermute | solution.py:146
  181.3 13.8 %collective-permute-start.34 = (bf16[32,3072]{1,0:T(8,128)(2,1)S(1)}, bf16[32,3072]{1,0:T(8,128)(2,1)S(1)}, u32[]{:S(2)}, u32[]{:S(2)}) collective-permute-start(bf16[32,3072]{1,0:T(8,128)(2,1)S(1)} %add_convert_fusion.3), channel_id=1, source_target_pairs={{0,3},{1,2},{2,1},{3,0},{4,7},{5,6},{6,5},{7,4},{8,11},{9,10},{10,... | collective-permute-start | bytes 589832 | tf_op jit(solution)/shard_map/ppermute | solution.py:146
  204.0 15.9 %collective-permute-start.37 = (bf16[32,3072]{1,0:T(8,128)(2,1)S(1)}, bf16[32,3072]{1,0:T(8,128)(2,1)S(1)}, u32[]{:S(2)}, u32[]{:S(2)}) collective-permute-start(bf16[32,3072]{1,0:T(8,128)(2,1)S(1)} %get-tuple-element.94), channel_id=1, source_target_pairs={{0,6},{1,7},{2,4},{3,5},{4,10},{5,11},{6,8},{7,9},{8,14},{9,15},{1... | collective-permute-start | bytes 589832 | tf_op jit(solution)/shard_map/ppermute | solution.py:146
  204.1 15.8 %collective-permute-start.38 = (bf16[32,3072]{1,0:T(8,128)(2,1)S(1)}, bf16[32,3072]{1,0:T(8,128)(2,1)S(1)}, u32[]{:S(2)}, u32[]{:S(2)}) collective-permute-start(bf16[32,3072]{1,0:T(8,128)(2,1)S(1)} %broadcast_select_fusion.1), channel_id=1, source_target_pairs={{0,7},{1,6},{2,5},{3,4},{4,11},{5,10},{6,9},{7,8},{8,15},{9,14},{1... | collective-permute-start | bytes 589832 | tf_op jit(solution)/shard_map/ppermute | solution.py:146
  204.6 17.0 %collective-permute-start.39 = (bf16[32,3072]{1,0:T(8,128)(2,1)S(1)}, bf16[32,3072]{1,0:T(8,128)(2,1)S(1)}, u32[]{:S(2)}, u32[]{:S(2)}) collective-permute-start(bf16[32,3072]{1,0:T(8,128)(2,1)S(1)} %get-tuple-element.93), channel_id=1, source_target_pairs={{0,5},{1,4},{2,7},{3,6},{4,9},{5,8},{6,11},{7,10},{8,13},{9,12},{1... | collective-permute-start | bytes 589832 | tf_op jit(solution)/shard_map/ppermute | solution.py:146
  206.0 15.6 %collective-permute-start.40 = (bf16[32,3072]{1,0:T(8,128)(2,1)S(1)}, bf16[32,3072]{1,0:T(8,128)(2,1)S(1)}, u32[]{:S(2)}, u32[]{:S(2)}) collective-permute-start(bf16[32,3072]{1,0:T(8,128)(2,1)S(1)} %add_convert_fusion.1), channel_id=1, source_target_pairs={{0,4},{1,5},{2,6},{3,7},{4,8},{5,9},{6,10},{7,11},{8,12},{9,13},{1... | collective-permute-start | bytes 589832 | tf_op jit(solution)/shard_map/ppermute | solution.py:146
  (10 other events, 69.3 us)

commit v2 on v1

--- a/solution.py
+++ b/solution.py
@@ -14,7 +14,6 @@
 VMEM_LIMIT = 12 * 2**20
 SCALE = HD ** (-0.5) * math.log2(math.e)
 OUT_STEPS = 3
-SHARES = (1, 1)
 
 
 def row_spans(refs):
@@ -168,10 +167,6 @@
     return lax.optimization_barrier((block, other))[0]
 
 
-def pieces_of(rows):
-    return [rows * share // sum(SHARES) for share in SHARES]
-
-
 def cut(blocks, sizes):
     whole = jnp.concatenate(blocks)
     starts = [sum(sizes[:i]) for i in range(len(sizes))]
@@ -186,7 +181,7 @@
     return kept, [jnp.where(low, near, last), jnp.where(low, last, near)]
 
 
-def passed_on(kept, terms, hop):
+def passed_on(kept, terms):
     count = len(kept)
     next_kept, next_others = [], []
     pair = None
@@ -194,8 +189,8 @@
         partners = partners if pair is None else behind(partners, pair)
         pair = rounded(mine, send(partners, NEAR))
         updated = rounded(current, pair, send(pair, FAR))
-        next_others.append(send(updated, NEAR, hop))
-        next_kept.append(send(updated, STAY, hop) if hop else updated)
+        next_others.append(send(updated, NEAR))
+        next_kept.append(updated)
     return next_kept, next_others
 
 
@@ -231,7 +226,6 @@
     )
     w, wo, kc, vc, gain = loaded(*stored)
     kept, others = gathered(state[0], low)
-    sizes = pieces_of(patch_rows // 2)
     for tick in range(TICKS):
         slot = patch_slot[(section_index - tick) % section_count]
         for index in range(PASSES):
@@ -239,12 +233,13 @@
             info = jnp.stack([slot * patch_rows, applies.astype(jnp.int32)])
             last = index == PASSES - 1
             final = last and tick == TICKS - 1
-            rows_out = [shard_rows] * n if final else sizes * 2
-            terms, kc, vc = block_terms(info, kept + others, rows_out, gain, w, wo, kc, vc)
+            terms, kc, vc = block_terms(info, kept + others, [shard_rows] * n, gain, w, wo, kc, vc)
             if final:
                 return delivered(kept, terms, low)[None]
-            kept = cut(kept, sizes) if tick + index == 0 else kept
-            kept, others = passed_on(kept, terms, 1 if last else 0)
+            if last:
+                kept, others = gathered(delivered(kept, terms, low), low)
+            else:
+                kept, others = passed_on(kept, terms)
 
 
 def solution(mesh):

time: 222 us -> 221 us (level)
  the two profiles are of different devices: /device:TPU:0 before, /device:TPU:14 now
where the time goes in v2:
time: 221 us
  waiting for transfers between devices  153 us (69%)
  starting transfers between devices  38.3 us (17%)
  Pallas kernels  22.2 us (10%)
  between operations  3.06 us (1%)
  other arithmetic  2.98 us (1%)
    ppermute x39, waiting for transfers between devices, send(): return lax.ppermute(block, ('section', 'uly'), route)  153 us
    ppermute x39, starting transfers between devices, send(): return lax.ppermute(block, ('section', 'uly'), route)  38.3 us
    pallas_call x6, Pallas kernels, block_terms(): pl.pallas_call(functools.partial(block_kernel, count, len(rows_out)), out...  18.2 us
  transfers between devices with their start and end apart: 39, of which 30 were waited for; matrix products, arithmetic and copies ran while one was open for 1% of the time, Pallas kernels for 2%

profile of v2, /device:TPU:14, one launch (start us, length us, event | category | flops | bytes accessed | tf_op | source)
XLA Modules:
  0.0 220.9 jit_solution(13879609115264042888)
XLA Ops:
  6.8 3.9 %shard_map.82 = (bf16[3072,1152]{1,0:T(8,128)(2,1)S(1)}, bf16[384,3072]{1,0:T(8,128)(2,1)S(1)}, bf16[512,384]{1,0:T(8,128)(2,1)S(1)}, bf16[512,384]{1,0:T(8,128)(2,1)S(1)}, bf16[1,3072]{1,0:T(2,128)(2,1)S(1)}) custom-call(bf16[3,3072,384]{2,1,0:T(8,128)(2,1)} %bitcast.11, bf16[384,3072]{1,0:T(8,128)(2,1)} %bitcast.12, bf16[512,384]{1,0:T(8,128)(2,1)} %bitcast.13, ...), custom_call_target="tpu_custom_call" | custom-call | bytes 10229760 | tf_op jit(solution)/shard_map/pallas_call | solution.py:94
  13.5 3.9 %collective-permute-done.2 = bf16[32,3072]{1,0:T(8,128)(2,1)S(1)} collective-permute-done((bf16[32,3072]{1,0:T(8,128)(2,1)S(1)}, bf16[32,3072]{1,0:T(8,128)(2,1)S(1)}, u32[]{:S(2)}, u32[]{:S(2)}) %collective-permute-start.2) | collective-permute-done | bytes 196640 | tf_op jit(solution)/shard_map/ppermute | solution.py:145
  17.4 3.0 %shard_map.83 = (bf16[32,3072]{1,0:T(8,128)(2,1)S(1)}, bf16[32,3072]{1,0:T(8,128)(2,1)S(1)}, bf16[32,3072]{1,0:T(8,128)(2,1)S(1)}, bf16[32,3072]{1,0:T(8,128)(2,...) custom-call(s32[2]{0:T(128)S(1)} %pad_add_fusion.4.info, ...), custom_call_target="tpu_custom_call", output_to_operand_aliasing={{4}: (8, {}), {5}: (9, {})} | custom-call | flops 1308622848 | bytes 9437184 | tf_op jit(solution)/shard_map/pallas_call | solution.py:114
  20.9 5.2 %collective-permute-done.3 = bf16[32,3072]{1,0:T(8,128)(2,1)S(1)} collective-permute-done((bf16[32,3072]{1,0:T(8,128)(2,1)S(1)}, bf16[32,3072]{1,0:T(8,128)(2,1)S(1)}, u32[]{:S(2)}, u32[]{:S(2)}) %collective-permute-start.3) | collective-permute-done | bytes 196640 | tf_op jit(solution)/shard_map/ppermute | solution.py:145
  28.0 6.1 %collective-permute-done.5 = bf16[32,3072]{1,0:T(8,128)(2,1)S(1)} collective-permute-done((bf16[32,3072]{1,0:T(8,128)(2,1)S(1)}, bf16[32,3072]{1,0:T(8,128)(2,1)S(1)}, u32[]{:S(2)}, u32[]{:S(2)}) %collective-permute-start.5) | collective-permute-done | bytes 196640 | tf_op jit(solution)/shard_map/ppermute | solution.py:145
  34.6 4.9 %collective-permute-done.4 = bf16[32,3072]{1,0:T(8,128)(2,1)S(1)} collective-permute-done((bf16[32,3072]{1,0:T(8,128)(2,1)S(1)}, bf16[32,3072]{1,0:T(8,128)(2,1)S(1)}, u32[]{:S(2)}, u32[]{:S(2)}) %collective-permute-start.4) | collective-permute-done | bytes 196640 | tf_op jit(solution)/shard_map/ppermute | solution.py:145
  39.7 4.3 %collective-permute-done.6 = bf16[32,3072]{1,0:T(8,128)(2,1)S(1)} collective-permute-done((bf16[32,3072]{1,0:T(8,128)(2,1)S(1)}, bf16[32,3072]{1,0:T(8,128)(2,1)S(1)}, u32[]{:S(2)}, u32[]{:S(2)}) %collective-permute-start.6) | collective-permute-done | bytes 196640 | tf_op jit(solution)/shard_map/ppermute | solution.py:145
  45.4 4.4 %collective-permute-done.8.refs_3_ = bf16[32,3072]{1,0:T(8,128)(2,1)S(1)} collective-permute-done((bf16[32,3072]{1,0:T(8,128)(2,1)S(1)}, bf16[32,3072]{1,0:T(8,128)(2,1)S(1)}, u32[]{:S(2)}, u32[]{:S(2)}) %collective-permute-start.8) | collective-permute-done | bytes 196640 | tf_op jit(solution)/shard_map/ppermute | solution.py:145
  56.4 13.9 %collective-permute-done.9 = bf16[32,3072]{1,0:T(8,128)(2,1)S(1)} collective-permute-done((bf16[32,3072]{1,0:T(8,128)(2,1)S(1)}, bf16[32,3072]{1,0:T(8,128)(2,1)S(1)}, u32[]{:S(2)}, u32[]{:S(2)}) %collective-permute-start.9) | collective-permute-done | bytes 196640 | tf_op jit(solution)/shard_map/ppermute | solution.py:145
  71.6 3.8 %collective-permute-start.14 = (bf16[32,3072]{1,0:T(8,128)(2,1)S(1)}, bf16[32,3072]{1,0:T(8,128)(2,1)S(1)}, u32[]{:S(2)}, u32[]{:S(2)}) collective-permute-start(bf16[32,3072]{1,0:T(8,128)(2,1)S(1)} %add_convert_fusion.12), channel_id=1, source_target_pairs={{0,1},{1,0},{2,3},{3,2},{4,5},{5,4},{6,7},{7,6},{8,9},{9,8},{10,11... | collective-permute-start | bytes 589832 | tf_op jit(solution)/shard_map/ppermute | solution.py:145
  75.3 6.4 %collective-permute-done.13 = bf16[32,3072]{1,0:T(8,128)(2,1)S(1)} collective-permute-done((bf16[32,3072]{1,0:T(8,128)(2,1)S(1)}, bf16[32,3072]{1,0:T(8,128)(2,1)S(1)}, u32[]{:S(2)}, u32[]{:S(2)}) %collective-permute-start.13) | collective-permute-done | bytes 196640 | tf_op jit(solution)/shard_map/ppermute | solution.py:145
  84.6 3.9 %collective-permute-done.15 = bf16[32,3072]{1,0:T(8,128)(2,1)S(1)} collective-permute-done((bf16[32,3072]{1,0:T(8,128)(2,1)S(1)}, bf16[32,3072]{1,0:T(8,128)(2,1)S(1)}, u32[]{:S(2)}, u32[]{:S(2)}) %collective-permute-start.15) | collective-permute-done | bytes 196640 | tf_op jit(solution)/shard_map/ppermute | solution.py:145
  88.5 3.0 %shard_map.85 = (bf16[32,3072]{1,0:T(8,128)(2,1)S(1)}, bf16[32,3072]{1,0:T(8,128)(2,1)S(1)}, bf16[32,3072]{1,0:T(8,128)(2,1)S(1)}, bf16[32,3072]{1,0:T(8,128)(2,...) custom-call(s32[2]{0:T(128)S(1)} %pad_add_fusion.2.info, ...), custom_call_target="tpu_custom_call", output_to_operand_aliasing={{4}: (8, {}), {5}: (9, {})} | custom-call | flops 1308622848 | bytes 9437184 | tf_op jit(solution)/shard_map/pallas_call | solution.py:114
  92.9 5.1 %collective-permute-done.16 = bf16[32,3072]{1,0:T(8,128)(2,1)S(1)} collective-permute-done((bf16[32,3072]{1,0:T(8,128)(2,1)S(1)}, bf16[32,3072]{1,0:T(8,128)(2,1)S(1)}, u32[]{:S(2)}, u32[]{:S(2)}) %collective-permute-start.16) | collective-permute-done | bytes 196640 | tf_op jit(solution)/shard_map/ppermute | solution.py:145
  101.1 4.9 %collective-permute-done.18 = bf16[32,3072]{1,0:T(8,128)(2,1)S(1)} collective-permute-done((bf16[32,3072]{1,0:T(8,128)(2,1)S(1)}, bf16[32,3072]{1,0:T(8,128)(2,1)S(1)}, u32[]{:S(2)}, u32[]{:S(2)}) %collective-permute-start.18) | collective-permute-done | bytes 196640 | tf_op jit(solution)/shard_map/ppermute | solution.py:145
  107.3 8.3 %collective-permute-done.17 = bf16[32,3072]{1,0:T(8,128)(2,1)S(1)} collective-permute-done((bf16[32,3072]{1,0:T(8,128)(2,1)S(1)}, bf16[32,3072]{1,0:T(8,128)(2,1)S(1)}, u32[]{:S(2)}, u32[]{:S(2)}) %collective-permute-start.17) | collective-permute-done | bytes 196640 | tf_op jit(solution)/shard_map/ppermute | solution.py:145
  118.5 4.8 %collective-permute-done.20.refs_2_ = bf16[32,3072]{1,0:T(8,128)(2,1)S(1)} collective-permute-done((bf16[32,3072]{1,0:T(8,128)(2,1)S(1)}, bf16[32,3072]{1,0:T(8,128)(2,1)S(1)}, u32[]{:S(2)}, u32[]{:S(2)}) %collective-permute-start.20) | collective-permute-done | bytes 196640 | tf_op jit(solution)/shard_map/ppermute | solution.py:145
  125.6 3.0 %shard_map.86 = (bf16[32,3072]{1,0:T(8,128)(2,1)S(1)}, bf16[32,3072]{1,0:T(8,128)(2,1)S(1)}, bf16[32,3072]{1,0:T(8,128)(2,1)S(1)}, bf16[32,3072]{1,0:T(8,128)(2,...) custom-call(s32[2]{0:T(128)S(1)} %pad_add_fusion.3.info, ...), custom_call_target="tpu_custom_call", output_to_operand_aliasing={{4}: (8, {}), {5}: (9, {})} | custom-call | flops 1308622848 | bytes 9437184 | tf_op jit(solution)/shard_map/pallas_call | solution.py:114
  128.8 5.2 %collective-permute-start.22 = (bf16[32,3072]{1,0:T(8,128)(2,1)S(1)}, bf16[32,3072]{1,0:T(8,128)(2,1)S(1)}, u32[]{:S(2)}, u32[]{:S(2)}) collective-permute-start(bf16[32,3072]{1,0:T(8,128)(2,1)S(1)} %get-tuple-element.96), channel_id=1, source_target_pairs={{0,6},{1,7},{2,4},{3,5},{4,10},{5,11},{6,8},{7,9},{8,14},{9,15},{1... | collective-permute-start | bytes 589832 | tf_op jit(solution)/shard_map/ppermute | solution.py:145
  134.3 10.2 %collective-permute-done.22 = bf16[32,3072]{1,0:T(8,128)(2,1)S(1)} collective-permute-done((bf16[32,3072]{1,0:T(8,128)(2,1)S(1)}, bf16[32,3072]{1,0:T(8,128)(2,1)S(1)}, u32[]{:S(2)}, u32[]{:S(2)}) %collective-permute-start.22) | collective-permute-done | bytes 196640 | tf_op jit(solution)/shard_map/ppermute | solution.py:145
  144.6 3.2 %collective-permute-start.26 = (bf16[32,3072]{1,0:T(8,128)(2,1)S(1)}, bf16[32,3072]{1,0:T(8,128)(2,1)S(1)}, u32[]{:S(2)}, u32[]{:S(2)}) collective-permute-start(bf16[32,3072]{1,0:T(8,128)(2,1)S(1)} %add_convert_fusion.6), channel_id=1, source_target_pairs={{0,3},{1,2},{2,1},{3,0},{4,7},{5,6},{6,5},{7,4},{8,11},{9,10},{10,... | collective-permute-start | bytes 589832 | tf_op jit(solution)/shard_map/ppermute | solution.py:145
  149.5 7.9 %collective-permute-done.26 = bf16[32,3072]{1,0:T(8,128)(2,1)S(1)} collective-permute-done((bf16[32,3072]{1,0:T(8,128)(2,1)S(1)}, bf16[32,3072]{1,0:T(8,128)(2,1)S(1)}, u32[]{:S(2)}, u32[]{:S(2)}) %collective-permute-start.26) | collective-permute-done | bytes 196640 | tf_op jit(solution)/shard_map/ppermute | solution.py:145
  158.6 5.5 %collective-permute-done.28 = bf16[32,3072]{1,0:T(8,128)(2,1)S(1)} collective-permute-done((bf16[32,3072]{1,0:T(8,128)(2,1)S(1)}, bf16[32,3072]{1,0:T(8,128)(2,1)S(1)}, u32[]{:S(2)}, u32[]{:S(2)}) %collective-permute-start.28) | collective-permute-done | bytes 196640 | tf_op jit(solution)/shard_map/ppermute | solution.py:145
  164.1 3.0 %shard_map.87 = (bf16[32,3072]{1,0:T(8,128)(2,1)S(1)}, bf16[32,3072]{1,0:T(8,128)(2,1)S(1)}, bf16[32,3072]{1,0:T(8,128)(2,1)S(1)}, bf16[32,3072]{1,0:T(8,128)(2,...) custom-call(s32[2]{0:T(128)S(1)} %pad_add_fusion.info, ...), custom_call_target="tpu_custom_call", output_to_operand_aliasing={{4}: (8, {}), {5}: (9, {})} | custom-call | flops 1308622848 | bytes 9437184 | tf_op jit(solution)/shard_map/pallas_call | solution.py:114
  168.3 5.0 %collective-permute-done.29 = bf16[32,3072]{1,0:T(8,128)(2,1)S(1)} collective-permute-done((bf16[32,3072]{1,0:T(8,128)(2,1)S(1)}, bf16[32,3072]{1,0:T(8,128)(2,1)S(1)}, u32[]{:S(2)}, u32[]{:S(2)}) %collective-permute-start.29) | collective-permute-done | bytes 196640 | tf_op jit(solution)/shard_map/ppermute | solution.py:145
  175.1 6.1 %collective-permute-done.31 = bf16[32,3072]{1,0:T(8,128)(2,1)S(1)} collective-permute-done((bf16[32,3072]{1,0:T(8,128)(2,1)S(1)}, bf16[32,3072]{1,0:T(8,128)(2,1)S(1)}, u32[]{:S(2)}, u32[]{:S(2)}) %collective-permute-start.31) | collective-permute-done | bytes 196640 | tf_op jit(solution)/shard_map/ppermute | solution.py:145
  182.1 6.3 %collective-permute-done.30 = bf16[32,3072]{1,0:T(8,128)(2,1)S(1)} collective-permute-done((bf16[32,3072]{1,0:T(8,128)(2,1)S(1)}, bf16[32,3072]{1,0:T(8,128)(2,1)S(1)}, u32[]{:S(2)}, u32[]{:S(2)}) %collective-permute-start.30) | collective-permute-done | bytes 196640 | tf_op jit(solution)/shard_map/ppermute | solution.py:145
  191.4 4.8 %collective-permute-start.34 = (bf16[32,3072]{1,0:T(8,128)(2,1)S(1)}, bf16[32,3072]{1,0:T(8,128)(2,1)S(1)}, u32[]{:S(2)}, u32[]{:S(2)}) collective-permute-start(bf16[32,3072]{1,0:T(8,128)(2,1)S(1)} %add_convert_fusion.2.refs_1_), channel_id=1, source_target_pairs={{0,1},{1,0},{2,3},{3,2},{4,5},{5,4},{6,7},{7,6},{8,9},{9,8},{10,11... | collective-permute-start | bytes 589832 | tf_op jit(solution)/shard_map/ppermute | solution.py:145
  196.2 3.6 %collective-permute-done.34.refs_3_ = bf16[32,3072]{1,0:T(8,128)(2,1)S(1)} collective-permute-done((bf16[32,3072]{1,0:T(8,128)(2,1)S(1)}, bf16[32,3072]{1,0:T(8,128)(2,1)S(1)}, u32[]{:S(2)}, u32[]{:S(2)}) %collective-permute-start.34) | collective-permute-done | bytes 196640 | tf_op jit(solution)/shard_map/ppermute | solution.py:145
  199.8 3.0 %shard_map.88 = (bf16[32,3072]{1,0:T(8,128)(2,1)S(1)}, bf16[32,3072]{1,0:T(8,128)(2,1)S(1)}, bf16[32,3072]{1,0:T(8,128)(2,1)S(1)}, bf16[32,3072]{1,0:T(8,128)(2,...) custom-call(s32[2]{0:T(128)S(1)} %pad_add_fusion.1.info, ...), custom_call_target="tpu_custom_call", output_to_operand_aliasing={{4}: (8, {}), {5}: (9, {})} | custom-call | flops 1308622848 | bytes 9437184 | tf_op jit(solution)/shard_map/pallas_call | solution.py:114
  203.3 11.0 %collective-permute-done.35 = bf16[32,3072]{1,0:T(8,128)(2,1)S(1)} collective-permute-done((bf16[32,3072]{1,0:T(8,128)(2,1)S(1)}, bf16[32,3072]{1,0:T(8,128)(2,1)S(1)}, u32[]{:S(2)}, u32[]{:S(2)}) %collective-permute-start.35) | collective-permute-done | bytes 196640 | tf_op jit(solution)/shard_map/ppermute | solution.py:145
  214.3 5.8 %collective-permute-done.36 = bf16[32,3072]{1,0:T(8,128)(2,1)S(1)} collective-permute-done((bf16[32,3072]{1,0:T(8,128)(2,1)S(1)}, bf16[32,3072]{1,0:T(8,128)(2,1)S(1)}, u32[]{:S(2)}, u32[]{:S(2)}) %collective-permute-start.36) | collective-permute-done | bytes 196640 | tf_op jit(solution)/shard_map/ppermute | solution.py:145
  (101 shorter events, 44.1 us)
Async XLA Ops:
  0.0 11.1 %collective-permute-start = (bf16[32,3072]{1,0:T(8,128)(2,1)}, bf16[32,3072]{1,0:T(8,128)(2,1)S(1)}, u32[]{:S(2)}, u32[]{:S(2)}) collective-permute-start(bf16[32,3072]{1,0:T(8,128)(2,1)} %bitcast.15), channel_id=1, source_target_pairs={{0,3},{1,2},{2,1},{3,0},{4,7},{5,6},{6,5},{7,4},{8,11},{9,10},{10,... | collective-permute-start | bytes 589832 | tf_op jit(solution)/shard_map/ppermute | solution.py:145
  1.6 11.9 %collective-permute-start.1 = (bf16[32,3072]{1,0:T(8,128)(2,1)}, bf16[32,3072]{1,0:T(8,128)(2,1)S(1)}, u32[]{:S(2)}, u32[]{:S(2)}) collective-permute-start(bf16[32,3072]{1,0:T(8,128)(2,1)} %bitcast.16), channel_id=1, source_target_pairs={{0,1},{1,0},{2,3},{3,2},{4,5},{5,4},{6,7},{7,6},{8,9},{9,8},{10,11... | collective-permute-start | bytes 589832 | tf_op jit(solution)/shard_map/ppermute | solution.py:145
  26.2 7.9 %collective-permute-start.5 = (bf16[32,3072]{1,0:T(8,128)(2,1)S(1)}, bf16[32,3072]{1,0:T(8,128)(2,1)S(1)}, u32[]{:S(2)}, u32[]{:S(2)}) collective-permute-start(bf16[32,3072]{1,0:T(8,128)(2,1)S(1)} %get-tuple-element.56), channel_id=1, source_target_pairs={{0,1},{1,0},{2,3},{3,2},{4,5},{5,4},{6,7},{7,6},{8,9},{9,8},{10,11... | collective-permute-start | bytes 589832 | tf_op jit(solution)/shard_map/ppermute | solution.py:145
  26.8 12.7 %collective-permute-start.4 = (bf16[32,3072]{1,0:T(8,128)(2,1)S(1)}, bf16[32,3072]{1,0:T(8,128)(2,1)S(1)}, u32[]{:S(2)}, u32[]{:S(2)}) collective-permute-start(bf16[32,3072]{1,0:T(8,128)(2,1)S(1)} %add_convert_fusion.17), channel_id=1, source_target_pairs={{0,3},{1,2},{2,1},{3,0},{4,7},{5,6},{6,5},{7,4},{8,11},{9,10},{10,... | collective-permute-start | bytes 589832 | tf_op jit(solution)/shard_map/ppermute | solution.py:145
  34.2 9.8 %collective-permute-start.6 = (bf16[32,3072]{1,0:T(8,128)(2,1)S(1)}, bf16[32,3072]{1,0:T(8,128)(2,1)S(1)}, u32[]{:S(2)}, u32[]{:S(2)}) collective-permute-start(bf16[32,3072]{1,0:T(8,128)(2,1)S(1)} %add_convert_fusion.15), channel_id=1, source_target_pairs={{0,3},{1,2},{2,1},{3,0},{4,7},{5,6},{6,5},{7,4},{8,11},{9,10},{10,... | collective-permute-start | bytes 589832 | tf_op jit(solution)/shard_map/ppermute | solution.py:145
  52.9 17.5 %collective-permute-start.10 = (bf16[32,3072]{1,0:T(8,128)(2,1)S(1)}, bf16[32,3072]{1,0:T(8,128)(2,1)S(1)}, u32[]{:S(2)}, u32[]{:S(2)}) collective-permute-start(bf16[32,3072]{1,0:T(8,128)(2,1)S(1)} %broadcast_select_fusion.15), channel_id=1, source_target_pairs={{0,7},{1,6},{2,5},{3,4},{4,11},{5,10},{6,9},{7,8},{8,15},{9,14},{1... | collective-permute-start | bytes 589832 | tf_op jit(solution)/shard_map/ppermute | solution.py:145
  53.0 17.3 %collective-permute-start.9 = (bf16[32,3072]{1,0:T(8,128)(2,1)S(1)}, bf16[32,3072]{1,0:T(8,128)(2,1)S(1)}, u32[]{:S(2)}, u32[]{:S(2)}) collective-permute-start(bf16[32,3072]{1,0:T(8,128)(2,1)S(1)} %get-tuple-element.102), channel_id=1, source_target_pairs={{0,6},{1,7},{2,4},{3,5},{4,10},{5,11},{6,8},{7,9},{8,14},{9,15},{1... | collective-permute-start | bytes 589832 | tf_op jit(solution)/shard_map/ppermute | solution.py:145
  55.2 15.3 %collective-permute-start.11 = (bf16[32,3072]{1,0:T(8,128)(2,1)S(1)}, bf16[32,3072]{1,0:T(8,128)(2,1)S(1)}, u32[]{:S(2)}, u32[]{:S(2)}) collective-permute-start(bf16[32,3072]{1,0:T(8,128)(2,1)S(1)} %get-tuple-element.101), channel_id=1, source_target_pairs={{0,5},{1,4},{2,7},{3,6},{4,9},{5,8},{6,11},{7,10},{8,13},{9,12},{1... | collective-permute-start | bytes 589832 | tf_op jit(solution)/shard_map/ppermute | solution.py:145
  56.4 14.1 %collective-permute-start.12 = (bf16[32,3072]{1,0:T(8,128)(2,1)S(1)}, bf16[32,3072]{1,0:T(8,128)(2,1)S(1)}, u32[]{:S(2)}, u32[]{:S(2)}) collective-permute-start(bf16[32,3072]{1,0:T(8,128)(2,1)S(1)} %add_convert_fusion.13), channel_id=1, source_target_pairs={{0,4},{1,5},{2,6},{3,7},{4,8},{5,9},{6,10},{7,11},{8,12},{9,13},{1... | collective-permute-start | bytes 589832 | tf_op jit(solution)/shard_map/ppermute | solution.py:145
  70.5 11.2 %collective-permute-start.13 = (bf16[32,3072]{1,0:T(8,128)(2,1)S(1)}, bf16[32,3072]{1,0:T(8,128)(2,1)S(1)}, u32[]{:S(2)}, u32[]{:S(2)}) collective-permute-start(bf16[32,3072]{1,0:T(8,128)(2,1)S(1)} %add_convert_fusion.12), channel_id=1, source_target_pairs={{0,3},{1,2},{2,1},{3,0},{4,7},{5,6},{6,5},{7,4},{8,11},{9,10},{10,... | collective-permute-start | bytes 589832 | tf_op jit(solution)/shard_map/ppermute | solution.py:145
  71.6 13.0 %collective-permute-start.14 = (bf16[32,3072]{1,0:T(8,128)(2,1)S(1)}, bf16[32,3072]{1,0:T(8,128)(2,1)S(1)}, u32[]{:S(2)}, u32[]{:S(2)}) collective-permute-start(bf16[32,3072]{1,0:T(8,128)(2,1)S(1)} %add_convert_fusion.12), channel_id=1, source_target_pairs={{0,1},{1,0},{2,3},{3,2},{4,5},{5,4},{6,7},{7,6},{8,9},{9,8},{10,11... | collective-permute-start | bytes 589832 | tf_op jit(solution)/shard_map/ppermute | solution.py:145
  81.7 6.8 %collective-permute-start.15 = (bf16[32,3072]{1,0:T(8,128)(2,1)S(1)}, bf16[32,3072]{1,0:T(8,128)(2,1)S(1)}, u32[]{:S(2)}, u32[]{:S(2)}) collective-permute-start(bf16[32,3072]{1,0:T(8,128)(2,1)S(1)} %collective-permute-done.13), channel_id=1, source_target_pairs={{0,1},{1,0},{2,3},{3,2},{4,5},{5,4},{6,7},{7,6},{8,9},{9,8},{10,11... | collective-permute-start | bytes 589832 | tf_op jit(solution)/shard_map/ppermute | solution.py:145
  98.0 7.9 %collective-permute-start.18 = (bf16[32,3072]{1,0:T(8,128)(2,1)S(1)}, bf16[32,3072]{1,0:T(8,128)(2,1)S(1)}, u32[]{:S(2)}, u32[]{:S(2)}) collective-permute-start(bf16[32,3072]{1,0:T(8,128)(2,1)S(1)} %get-tuple-element.69), channel_id=1, source_target_pairs={{0,1},{1,0},{2,3},{3,2},{4,5},{5,4},{6,7},{7,6},{8,9},{9,8},{10,11... | collective-permute-start | bytes 589832 | tf_op jit(solution)/shard_map/ppermute | solution.py:145
  99.9 15.7 %collective-permute-start.17 = (bf16[32,3072]{1,0:T(8,128)(2,1)S(1)}, bf16[32,3072]{1,0:T(8,128)(2,1)S(1)}, u32[]{:S(2)}, u32[]{:S(2)}) collective-permute-start(bf16[32,3072]{1,0:T(8,128)(2,1)S(1)} %add_convert_fusion.11), channel_id=1, source_target_pairs={{0,3},{1,2},{2,1},{3,0},{4,7},{5,6},{6,5},{7,4},{8,11},{9,10},{10,... | collective-permute-start | bytes 589832 | tf_op jit(solution)/shard_map/ppermute | solution.py:145
  106.0 12.2 %collective-permute-start.19 = (bf16[32,3072]{1,0:T(8,128)(2,1)S(1)}, bf16[32,3072]{1,0:T(8,128)(2,1)S(1)}, u32[]{:S(2)}, u32[]{:S(2)}) collective-permute-start(bf16[32,3072]{1,0:T(8,128)(2,1)S(1)} %add_convert_fusion.9), channel_id=1, source_target_pairs={{0,3},{1,2},{2,1},{3,0},{4,7},{5,6},{6,5},{7,4},{8,11},{9,10},{10,... | collective-permute-start | bytes 589832 | tf_op jit(solution)/shard_map/ppermute | solution.py:145
  115.7 7.6 %collective-permute-start.20 = (bf16[32,3072]{1,0:T(8,128)(2,1)S(1)}, bf16[32,3072]{1,0:T(8,128)(2,1)S(1)}, u32[]{:S(2)}, u32[]{:S(2)}) collective-permute-start(bf16[32,3072]{1,0:T(8,128)(2,1)S(1)} %add_convert_fusion.10.refs_0_), channel_id=1, source_target_pairs={{0,1},{1,0},{2,3},{3,2},{4,5},{5,4},{6,7},{7,6},{8,9},{9,8},{10,11... | collective-permute-start | bytes 589832 | tf_op jit(solution)/shard_map/ppermute | solution.py:145
  118.3 7.3 %collective-permute-start.21 = (bf16[32,3072]{1,0:T(8,128)(2,1)S(1)}, bf16[32,3072]{1,0:T(8,128)(2,1)S(1)}, u32[]{:S(2)}, u32[]{:S(2)}) collective-permute-start(bf16[32,3072]{1,0:T(8,128)(2,1)S(1)} %add_convert_fusion.8.refs_1_), channel_id=1, source_target_pairs={{0,1},{1,0},{2,3},{3,2},{4,5},{5,4},{6,7},{7,6},{8,9},{9,8},{10,11... | collective-permute-start | bytes 589832 | tf_op jit(solution)/shard_map/ppermute | solution.py:145
  128.7 15.8 %collective-permute-start.23 = (bf16[32,3072]{1,0:T(8,128)(2,1)S(1)}, bf16[32,3072]{1,0:T(8,128)(2,1)S(1)}, u32[]{:S(2)}, u32[]{:S(2)}) collective-permute-start(bf16[32,3072]{1,0:T(8,128)(2,1)S(1)} %broadcast_select_fusion.7), channel_id=1, source_target_pairs={{0,7},{1,6},{2,5},{3,4},{4,11},{5,10},{6,9},{7,8},{8,15},{9,14},{1... | collective-permute-start | bytes 589832 | tf_op jit(solution)/shard_map/ppermute | solution.py:145
  128.8 15.6 %collective-permute-start.22 = (bf16[32,3072]{1,0:T(8,128)(2,1)S(1)}, bf16[32,3072]{1,0:T(8,128)(2,1)S(1)}, u32[]{:S(2)}, u32[]{:S(2)}) collective-permute-start(bf16[32,3072]{1,0:T(8,128)(2,1)S(1)} %get-tuple-element.96), channel_id=1, source_target_pairs={{0,6},{1,7},{2,4},{3,5},{4,10},{5,11},{6,8},{7,9},{8,14},{9,15},{1... | collective-permute-start | bytes 589832 | tf_op jit(solution)/shard_map/ppermute | solution.py:145
  134.1 10.4 %collective-permute-start.24 = (bf16[32,3072]{1,0:T(8,128)(2,1)S(1)}, bf16[32,3072]{1,0:T(8,128)(2,1)S(1)}, u32[]{:S(2)}, u32[]{:S(2)}) collective-permute-start(bf16[32,3072]{1,0:T(8,128)(2,1)S(1)} %get-tuple-element.95), channel_id=1, source_target_pairs={{0,5},{1,4},{2,7},{3,6},{4,9},{5,8},{6,11},{7,10},{8,13},{9,12},{1... | collective-permute-start | bytes 589832 | tf_op jit(solution)/shard_map/ppermute | solution.py:145
  134.2 10.4 %collective-permute-start.25 = (bf16[32,3072]{1,0:T(8,128)(2,1)S(1)}, bf16[32,3072]{1,0:T(8,128)(2,1)S(1)}, u32[]{:S(2)}, u32[]{:S(2)}) collective-permute-start(bf16[32,3072]{1,0:T(8,128)(2,1)S(1)} %add_convert_fusion.7), channel_id=1, source_target_pairs={{0,4},{1,5},{2,6},{3,7},{4,8},{5,9},{6,10},{7,11},{8,12},{9,13},{1... | collective-permute-start | bytes 589832 | tf_op jit(solution)/shard_map/ppermute | solution.py:145
  144.6 12.8 %collective-permute-start.26 = (bf16[32,3072]{1,0:T(8,128)(2,1)S(1)}, bf16[32,3072]{1,0:T(8,128)(2,1)S(1)}, u32[]{:S(2)}, u32[]{:S(2)}) collective-permute-start(bf16[32,3072]{1,0:T(8,128)(2,1)S(1)} %add_convert_fusion.6), channel_id=1, source_target_pairs={{0,3},{1,2},{2,1},{3,0},{4,7},{5,6},{6,5},{7,4},{8,11},{9,10},{10,... | collective-permute-start | bytes 589832 | tf_op jit(solution)/shard_map/ppermute | solution.py:145
  148.6 10.0 %collective-permute-start.27 = (bf16[32,3072]{1,0:T(8,128)(2,1)S(1)}, bf16[32,3072]{1,0:T(8,128)(2,1)S(1)}, u32[]{:S(2)}, u32[]{:S(2)}) collective-permute-start(bf16[32,3072]{1,0:T(8,128)(2,1)S(1)} %add_convert_fusion.6), channel_id=1, source_target_pairs={{0,1},{1,0},{2,3},{3,2},{4,5},{5,4},{6,7},{7,6},{8,9},{9,8},{10,11... | collective-permute-start | bytes 589832 | tf_op jit(solution)/shard_map/ppermute | solution.py:145
  173.3 7.9 %collective-permute-start.31 = (bf16[32,3072]{1,0:T(8,128)(2,1)S(1)}, bf16[32,3072]{1,0:T(8,128)(2,1)S(1)}, u32[]{:S(2)}, u32[]{:S(2)}) collective-permute-start(bf16[32,3072]{1,0:T(8,128)(2,1)S(1)} %get-tuple-element.82), channel_id=1, source_target_pairs={{0,1},{1,0},{2,3},{3,2},{4,5},{5,4},{6,7},{7,6},{8,9},{9,8},{10,11... | collective-permute-start | bytes 589832 | tf_op jit(solution)/shard_map/ppermute | solution.py:145
  175.1 13.3 %collective-permute-start.30 = (bf16[32,3072]{1,0:T(8,128)(2,1)S(1)}, bf16[32,3072]{1,0:T(8,128)(2,1)S(1)}, u32[]{:S(2)}, u32[]{:S(2)}) collective-permute-start(bf16[32,3072]{1,0:T(8,128)(2,1)S(1)} %add_convert_fusion.5), channel_id=1, source_target_pairs={{0,3},{1,2},{2,1},{3,0},{4,7},{5,6},{6,5},{7,4},{8,11},{9,10},{10,... | collective-permute-start | bytes 589832 | tf_op jit(solution)/shard_map/ppermute | solution.py:145
  181.3 10.0 %collective-permute-start.32 = (bf16[32,3072]{1,0:T(8,128)(2,1)S(1)}, bf16[32,3072]{1,0:T(8,128)(2,1)S(1)}, u32[]{:S(2)}, u32[]{:S(2)}) collective-permute-start(bf16[32,3072]{1,0:T(8,128)(2,1)S(1)} %add_convert_fusion.3), channel_id=1, source_target_pairs={{0,3},{1,2},{2,1},{3,0},{4,7},{5,6},{6,5},{7,4},{8,11},{9,10},{10,... | collective-permute-start | bytes 589832 | tf_op jit(solution)/shard_map/ppermute | solution.py:145
  188.5 7.7 %collective-permute-start.33 = (bf16[32,3072]{1,0:T(8,128)(2,1)S(1)}, bf16[32,3072]{1,0:T(8,128)(2,1)S(1)}, u32[]{:S(2)}, u32[]{:S(2)}) collective-permute-start(bf16[32,3072]{1,0:T(8,128)(2,1)S(1)} %add_convert_fusion.4.refs_0_), channel_id=1, source_target_pairs={{0,1},{1,0},{2,3},{3,2},{4,5},{5,4},{6,7},{7,6},{8,9},{9,8},{10,11... | collective-permute-start | bytes 589832 | tf_op jit(solution)/shard_map/ppermute | solution.py:145
  191.4 8.4 %collective-permute-start.34 = (bf16[32,3072]{1,0:T(8,128)(2,1)S(1)}, bf16[32,3072]{1,0:T(8,128)(2,1)S(1)}, u32[]{:S(2)}, u32[]{:S(2)}) collective-permute-start(bf16[32,3072]{1,0:T(8,128)(2,1)S(1)} %add_convert_fusion.2.refs_1_), channel_id=1, source_target_pairs={{0,1},{1,0},{2,3},{3,2},{4,5},{5,4},{6,7},{7,6},{8,9},{9,8},{10,11... | collective-permute-start | bytes 589832 | tf_op jit(solution)/shard_map/ppermute | solution.py:145
  202.9 11.4 %collective-permute-start.35 = (bf16[32,3072]{1,0:T(8,128)(2,1)S(1)}, bf16[32,3072]{1,0:T(8,128)(2,1)S(1)}, u32[]{:S(2)}, u32[]{:S(2)}) collective-permute-start(bf16[32,3072]{1,0:T(8,128)(2,1)S(1)} %get-tuple-element.90), channel_id=1, source_target_pairs={{0,6},{1,7},{2,4},{3,5},{4,10},{5,11},{6,8},{7,9},{8,14},{9,15},{1... | collective-permute-start | bytes 589832 | tf_op jit(solution)/shard_map/ppermute | solution.py:145
  203.0 17.1 %collective-permute-start.36 = (bf16[32,3072]{1,0:T(8,128)(2,1)S(1)}, bf16[32,3072]{1,0:T(8,128)(2,1)S(1)}, u32[]{:S(2)}, u32[]{:S(2)}) collective-permute-start(bf16[32,3072]{1,0:T(8,128)(2,1)S(1)} %broadcast_select_fusion), channel_id=1, source_target_pairs={{0,7},{1,6},{2,5},{3,4},{4,11},{5,10},{6,9},{7,8},{8,15},{9,14},{1... | collective-permute-start | bytes 589832 | tf_op jit(solution)/shard_map/ppermute | solution.py:145
  203.2 16.9 %collective-permute-start.37 = (bf16[32,3072]{1,0:T(8,128)(2,1)S(1)}, bf16[32,3072]{1,0:T(8,128)(2,1)S(1)}, u32[]{:S(2)}, u32[]{:S(2)}) collective-permute-start(bf16[32,3072]{1,0:T(8,128)(2,1)S(1)} %get-tuple-element.89), channel_id=1, source_target_pairs={{0,5},{1,4},{2,7},{3,6},{4,9},{5,8},{6,11},{7,10},{8,13},{9,12},{1... | collective-permute-start | bytes 589832 | tf_op jit(solution)/shard_map/ppermute | solution.py:145
  203.2 16.9 %collective-permute-start.38 = (bf16[32,3072]{1,0:T(8,128)(2,1)S(1)}, bf16[32,3072]{1,0:T(8,128)(2,1)S(1)}, u32[]{:S(2)}, u32[]{:S(2)}) collective-permute-start(bf16[32,3072]{1,0:T(8,128)(2,1)S(1)} %add_convert_fusion.1), channel_id=1, source_target_pairs={{0,4},{1,5},{2,6},{3,7},{4,8},{5,9},{6,10},{7,11},{8,12},{9,13},{1... | collective-permute-start | bytes 589832 | tf_op jit(solution)/shard_map/ppermute | solution.py:145
  (8 other events, 53.9 us)
